TPU v7x, 32 devices: a whole 2x2x4 slice. The times are simulated.
32 devices in a mesh: genome: 8 (over z, x), samp: 4 (over y, core).
Axes of the slice: x: 2, y: 2, z: 4, core: 2. Of those that a mesh axis runs over, the one named last changes fastest.
Arguments:
- dosage: bfloat16 [16384, 8192], P('samp', 'genome'), may hold values from -6 to 6
- effects: bfloat16 [8192, 512], P('genome', 'samp'), may hold values from -6 to 6
- depth: int32 [32], P('genome'), may hold values from 1 to 4
Outputs:
- ld_effects: float32 [8192, 512], P('genome', 'samp')
Inputs may be any that keep to these rules, and one draw needn't show every extreme that they name: Every block's window depth lies between 1 and 4.
All inputs are finite; a program needn't handle non-finite values.
Results may differ from a plain program's by a relative error of at most 0.0029.
Values may be sent and summed in bfloat16 or wider, within the bound.
A program may use at most 128 MiB of HBM per device.

v0:
```python
import functools

import jax
import jax.numpy as jnp
from jax import lax
from jax.experimental import pallas as pl
from jax.experimental.pallas import tpu as pltpu
from jax.sharding import PartitionSpec as P

BLK = 256
MESH = pl.DeviceIdType.MESH
F32 = jnp.float32
BF16 = jnp.bfloat16
CONTRACT0 = (((0,), (0,)), ((), ()))


def gram(left, right):
    return lax.dot_general(left, right, CONTRACT0, preferred_element_type=F32)


def kernel(
    n_genome, n_samp, nb, half, traits, scale,
    x_ref, e_ref, depth_ref, out_ref,
    d_ref, own, xbuf, zbuf, eff, dep, loc, cro, par, far, lc_in, ly_out, ly_in, c_in, y_out, y_in, hop_out, hop_in,
    own_sem, own_e_sem, x_send, x_recv, z_send, z_recv, es_send, es_recv, ex_send, ex_recv,
    ds_send, ds_recv, lc_send, lc_recv, ly_send, ly_recv, c_send, c_recv, y_send, y_recv, h_send, h_recv,
):
    g = lax.axis_index("genome")
    s = lax.axis_index("samp")
    q = lax.rem(g, 2)
    sign = 1 - 2 * q
    partner = g + sign
    z_from = g + 2 * sign
    z_to = g - 2 * sign
    has_from = jnp.logical_and(z_from >= 0, z_from < n_genome)
    has_to = jnp.logical_and(z_to >= 0, z_to < n_genome)

    def mine(u):
        return u + q * (nb - 1 - 2 * u)

    def other(u):
        return nb - 1 - mine(u)

    core = lax.rem(s, 2)
    core_mate = s + 1 - 2 * core
    cross_mate = lax.rem(s + 2, n_samp)

    def cols(t):
        return pl.ds(pl.multiple_of(t * traits, traits), traits)

    my_cols = cols(s)
    keep_rows = pl.ds(pl.multiple_of(q * half, half), half)
    give_rows = pl.ds(pl.multiple_of((1 - q) * half, half), half)

    def remote(src, dst, ss, rsem, gg, sss):
        return pltpu.make_async_remote_copy(
            src_ref=src, dst_ref=dst, send_sem=ss, recv_sem=rsem,
            device_id=(gg, sss), device_id_type=MESH,
        )

    barrier = pltpu.get_barrier_semaphore()
    for mate in (core_mate, cross_mate):
        pl.semaphore_signal(barrier, inc=1, device_id=(g, mate), device_id_type=MESH)
    pl.semaphore_signal(barrier, inc=1, device_id=(partner, s), device_id_type=MESH)

    @pl.when(has_from)
    def _():
        pl.semaphore_signal(barrier, inc=1, device_id=(z_from, s), device_id_type=MESH)

    @pl.when(has_to)
    def _():
        pl.semaphore_signal(barrier, inc=1, device_id=(z_to, s), device_id_type=MESH)

    own_copies = [
        pltpu.make_async_copy(x_ref.at[:, b * BLK : (b + 1) * BLK], own.at[b], own_sem.at[b])
        for b in range(nb)
    ]
    own_e = pltpu.make_async_copy(e_ref, eff.at[0, :, my_cols], own_e_sem.at[0])
    own_e.start()
    for c in own_copies:
        c.start()
    pl.semaphore_wait(
        barrier, 3 + has_from.astype(jnp.int32) + has_to.astype(jnp.int32)
    )

    for b in range(nb):
        d_ref[b : b + 1, :] = jnp.full((1, BLK), depth_ref[b].astype(F32))

    def block_cols(b):
        return pl.ds(pl.multiple_of(b * BLK, BLK), BLK)

    x_copies = [
        remote(x_ref.at[give_rows, block_cols(other(t))], xbuf.at[t], x_send.at[t], x_recv.at[t], partner, s)
        for t in range(nb)
    ]
    z_copies = [
        remote(x_ref.at[keep_rows, block_cols(mine(t))], zbuf.at[t], z_send.at[t], z_recv.at[t], z_to, s)
        for t in range(nb)
    ]
    d_x = remote(d_ref, dep.at[0], ds_send.at[0], ds_recv.at[0], partner, s)
    d_z = remote(d_ref, dep.at[1], ds_send.at[1], ds_recv.at[1], z_to, s)
    e_x = remote(e_ref, eff.at[1, :, my_cols], ex_send.at[0], ex_recv.at[0], partner, s)
    e_z = remote(e_ref, eff.at[2, :, my_cols], ex_send.at[1], ex_recv.at[1], z_to, s)
    d_x.start()
    e_x.start()
    x_copies[0].start()
    x_copies[1].start()

    @pl.when(has_to)
    def _():
        d_z.start()
        e_z.start()
        z_copies[0].start()
        z_copies[1].start()

    def gather(slot, source):
        across = cols(cross_mate)
        here = eff.at[slot, :, my_cols]
        there = eff.at[slot, :, across]
        return [
            remote(source, here, es_send.at[slot, 0], es_recv.at[slot, 0], g, core_mate),
            remote(source, here, es_send.at[slot, 1], es_recv.at[slot, 1], g, cross_mate),
            remote(there, there, es_send.at[slot, 2], es_recv.at[slot, 2], g, core_mate),
        ]

    e_own = gather(0, e_ref)
    e_partner = gather(1, eff.at[1, :, my_cols])
    e_far = gather(2, eff.at[2, :, my_cols])
    e_own[0].start()
    e_own[1].start()
    loc[...] = jnp.zeros_like(loc)
    cro[...] = jnp.zeros_like(cro)
    par[...] = jnp.zeros_like(par)
    far[...] = jnp.zeros_like(far)
    e_own[1].wait_recv()
    e_own[2].start()
    e_x.wait_recv()
    e_partner[0].start()
    e_partner[1].start()

    @pl.when(has_from)
    def _():
        e_z.wait_recv()
        e_far[0].start()
        e_far[1].start()

    own_e.wait()
    for c in own_copies:
        c.wait()
    e_own[0].wait_recv()
    e_own[2].wait_recv()

    def weight(drow, k):
        return jnp.where(drow >= k.astype(F32), F32(scale), F32(0.0))

    def rows(b):
        return pl.ds(pl.multiple_of(b * BLK, BLK), BLK)

    def local_row(i, carry):
        def local_pair(j, carry):
            full = gram(own[i, :half], own[j, :half]) + gram(own[i, half:], own[j, half:])
            full = full * weight(d_ref[pl.ds(i, 1), :], j - i)
            high = full.astype(BF16)
            low = (full - high.astype(F32)).astype(BF16)
            ej = eff[0, rows(j), :]
            loc[rows(i), :] += jnp.dot(high, ej, preferred_element_type=F32) + jnp.dot(
                low, ej, preferred_element_type=F32
            )

            @pl.when(j > i)
            def _():
                ei = eff[0, rows(i), :]
                loc[rows(j), :] += gram(high, ei) + gram(low, ei)

            return carry

        return lax.fori_loop(i, nb, local_pair, carry)

    lax.fori_loop(0, nb, local_row, 0)
    def loc_core(y):
        return remote(
            loc.at[:, cols(2 * y + 1 - core)], lc_in.at[y], lc_send.at[y], lc_recv.at[y], g, core_mate
        )

    loc_across = remote(ly_out, ly_in, ly_send.at[0], ly_recv.at[0], g, cross_mate)
    loc_core(0).start()
    loc_core(1).start()
    e_partner[1].wait_recv()
    e_partner[2].start()
    d_x.wait_recv()

    @pl.when(has_from)
    def _():
        e_far[1].wait_recv()
        e_far[2].start()
        d_z.wait_recv()

    my_y = s // 2
    mate_y = 1 - my_y
    loc_core(0).wait_recv()
    loc_core(1).wait_recv()
    ly_out[...] = loc[:, cols(cross_mate)] + lc_in[mate_y]
    loc_across.start()
    e_partner[0].wait_recv()
    e_partner[2].wait_recv()

    @pl.when(has_from)
    def _():
        e_far[0].wait_recv()
        e_far[2].wait_recv()

    kinds = {"own": (0, cro), "partner": (1, par), "far": (2, far)}

    def block_rows(t):
        return pl.ds(t * BLK, BLK)

    def to_core(kind, t):
        n, acc = kinds[kind]
        return [
            remote(
                acc.at[block_rows(t), cols(2 * y + 1 - core)], c_in.at[n, t, y],
                c_send.at[n, t, y], c_recv.at[n, t, y], g, core_mate,
            )
            for y in range(2)
        ]

    def across(kind, t):
        n, _ = kinds[kind]
        return remote(y_out.at[n, t], y_in.at[n, t], y_send.at[n, t], y_recv.at[n, t], g, cross_mate)

    def publish(kind, t):
        for c in to_core(kind, t):
            c.start()

    def relay(kind, t):
        n, acc = kinds[kind]
        for c in to_core(kind, t):
            c.wait_recv()
        y_out[n, t] = (acc[block_rows(t), cols(cross_mate)] + c_in[n, t, mate_y]).astype(BF16)
        across(kind, t).start()

    def collect(kind, t):
        n, acc = kinds[kind]
        across(kind, t).wait_recv()
        return acc[block_rows(t), my_cols] + c_in[n, t, my_y] + y_in[n, t].astype(F32)

    def hop(n, t):
        return remote(
            hop_out.at[n, t], hop_in.at[n, t], h_send.at[n, t], h_recv.at[n, t],
            partner if n == 0 else z_from, s,
        )

    def prepare(n, t):
        hop_out[n, t] = collect("partner" if n == 0 else "far", t).astype(BF16)

    def forward(n, t):
        prepare(n, t)
        hop(n, t).start()

    for t in range(nb):
        x_copies[t].wait_recv()
        if t == nb - 1:
            for j in range(nb - 2):
                hop(0, j).start()
        if t + 2 < nb:
            x_copies[t].wait_send()
            x_copies[t + 2].start()

            @pl.when(has_to)
            def _():
                z_copies[t].wait_send()
                z_copies[t + 2].start()

        def x_pair(u, carry):
            k = nb + t - u
            mu, mt = mine(u), mine(t)
            drow = jnp.where(q == 0, d_ref[pl.ds(mu, 1), :], dep[0, pl.ds(mt, 1), :])
            full = gram(own[mu, keep_rows, :], xbuf[t]) * weight(drow, k)
            high = full.astype(BF16)
            cro[rows(u), :] += jnp.dot(high, eff[1, rows(other(nb - 1 - t)), :], preferred_element_type=F32)
            par[t * BLK : (t + 1) * BLK, :] += gram(high, eff[0, rows(mu), :])
            return carry

        if t > 0:
            relay("partner", t - 1)
            relay("own", t - 1)

        if t == nb - 1:
            x_pair(jnp.int32(t), 0)
            publish("own", t)

        @pl.when(has_from)
        def _():
            if t < nb - 1:
                z_copies[t].wait_recv()

            def z_pair(v, carry):
                k = nb + v - t
                mt, mv = mine(t), mine(v)
                drow = jnp.where(q == 0, dep[0, pl.ds(mt, 1), :], dep[1, pl.ds(mv, 1), :])
                full = gram(xbuf[t], zbuf[v]) * weight(drow, jnp.int32(0) + k)
                high = full.astype(BF16)
                par[t * BLK : (t + 1) * BLK, :] += jnp.dot(high, eff[2, rows(mv), :], preferred_element_type=F32)
                far[rows(v), :] += gram(high, eff[1, rows(mt), :])
                return carry

            if t < nb - 1:
                lax.fori_loop(0, t + 1, z_pair, 0)
            else:
                for v in range(nb):
                    if v == t:
                        z_copies[t].wait_recv()
                    z_pair(jnp.int32(v), 0)
                    publish("far", v)
                    if v > 0:
                        relay("far", v - 1)

        if t < nb - 1:
            lax.fori_loop(t, nb, x_pair, 0)
        publish("partner", t)
        if t < nb - 1:
            publish("own", t)
        if 0 < t < nb - 1:
            prepare(0, t - 1)

    @pl.when(has_from)
    def _():
        relay("far", nb - 1)

    relay("partner", nb - 1)
    relay("own", nb - 1)
    forward(0, nb - 2)

    @pl.when(has_from)
    def _():
        for v in range(nb - 1):
            forward(1, v)

    loc_across.wait_recv()
    out_ref[...] = loc[:, my_cols] + lc_in[my_y] + ly_in[...]
    for t in range(nb - 1):
        out_ref[rows(mine(t)), :] += collect("own", t)

    @pl.when(has_from)
    def _():
        forward(1, nb - 1)

    forward(0, nb - 1)
    out_ref[rows(mine(nb - 1)), :] += collect("own", nb - 1)
    for t in range(nb):
        hop(0, t).wait_recv()
        out_ref[rows(other(t)), :] += hop_in[0, t].astype(F32)

    @pl.when(has_to)
    def _():
        for v in range(nb):
            hop(1, v).wait_recv()
            out_ref[rows(mine(v)), :] += hop_in[1, v].astype(F32)

    d_x.wait_send()
    e_x.wait_send()
    for t in range(nb - 2, nb):
        x_copies[t].wait_send()

    @pl.when(has_to)
    def _():
        d_z.wait_send()
        e_z.wait_send()
        for t in range(nb - 2, nb):
            z_copies[t].wait_send()

    for c in e_own + e_partner + [loc_core(0), loc_core(1), loc_across]:
        c.wait_send()
    for t in range(nb):
        for kind in ("own", "partner"):
            for c in to_core(kind, t) + [across(kind, t)]:
                c.wait_send()
        hop(0, t).wait_send()

    @pl.when(has_from)
    def _():
        for c in e_far:
            c.wait_send()
        for t in range(nb):
            for c in to_core("far", t) + [across("far", t)]:
                c.wait_send()
            hop(1, t).wait_send()


def body(n_genome, n_samp, dosage, effects, depth):
    nb = depth.shape[0]
    samples, variants = dosage.shape
    traits = effects.shape[1]
    all_traits = traits * n_samp
    half = samples // 2
    dma = pltpu.SemaphoreType.DMA
    return pl.pallas_call(
        functools.partial(kernel, n_genome, n_samp, nb, half, traits, 1.0 / (samples * n_samp)),
        out_shape=jax.ShapeDtypeStruct((variants, traits), F32),
        in_specs=[
            pl.BlockSpec(memory_space=pl.ANY),
            pl.BlockSpec(memory_space=pl.ANY),
            pl.BlockSpec(memory_space=pltpu.SMEM),
        ],
        out_specs=pl.BlockSpec(memory_space=pltpu.VMEM),
        scratch_shapes=[
            pltpu.VMEM((8, BLK), F32),
            pltpu.VMEM((nb, samples, BLK), BF16),
            pltpu.VMEM((nb, half, BLK), BF16),
            pltpu.VMEM((nb, half, BLK), BF16),
            pltpu.VMEM((3, variants, all_traits), BF16),
            pltpu.VMEM((2, 8, BLK), F32),
            pltpu.VMEM((variants, all_traits), F32),
            pltpu.VMEM((variants, all_traits), F32),
            pltpu.VMEM((variants, all_traits), F32),
            pltpu.VMEM((variants, all_traits), F32),
            pltpu.VMEM((2, variants, traits), F32),
            pltpu.VMEM((variants, traits), F32),
            pltpu.VMEM((variants, traits), F32),
            pltpu.VMEM((3, nb, 2, BLK, traits), F32),
            pltpu.VMEM((3, nb, BLK, traits), BF16),
            pltpu.VMEM((3, nb, BLK, traits), BF16),
            pltpu.VMEM((2, nb, BLK, traits), BF16),
            pltpu.VMEM((2, nb, BLK, traits), BF16),
            dma((nb,)), dma((1,)),
            dma((nb,)), dma((nb,)), dma((nb,)), dma((nb,)),
            dma((3, 3)), dma((3, 3)),
            dma((2,)), dma((2,)), dma((2,)), dma((2,)),
            dma((2,)), dma((2,)), dma((1,)), dma((1,)),
            dma((3, nb, 2)), dma((3, nb, 2)), dma((3, nb)), dma((3, nb)),
            dma((2, nb)), dma((2, nb)),
        ],
        compiler_params=pltpu.CompilerParams(
            collective_id=0, has_side_effects=True, vmem_limit_bytes=60 * 1024 * 1024
        ),
        cost_estimate=pl.CostEstimate(
            flops=2 * 20 * BLK * BLK * samples, bytes_accessed=4 * samples * variants, transcendentals=0
        ),
    )(dosage, effects, depth)


def solution(mesh):
    return jax.shard_map(
        functools.partial(body, mesh.shape["genome"], mesh.shape["samp"]),
        mesh=mesh,
        in_specs=(P("samp", "genome"), P("genome", "samp"), P("genome")),
        out_specs=P("genome", "samp"),
        check_vma=False,
    )
```

profile of v0, /device:TPU:0, one launch (start us, length us, event | category | flops | bytes accessed | tf_op | source)
XLA Modules:
  0.0 120.3 jit_solution(13575513131529145387)
XLA Ops:
  0.0 118.4 %shard_map.37 = f32[1024,128]{1,0:T(8,128)} custom-call(bf16[4096,1024]{1,0:T(8,128)(2,1)} %x_ref.1, bf16[1024,128]{1,0:T(8,128)(2,1)} %e_ref.1, s32[4]{0:T(128)} %depth_ref.1), custom_call_target="tpu_custom_call" | custom-call | flops 10737418240 | bytes 16777216 | tf_op jit(solution)/shard_map/pallas_call | solution.py:397
  118.5 1.9 %copy.5 = f32[1024,128]{1,0:T(8,128)} copy(f32[1024,128]{1,0:T(8,128)} %shard_map.37) | data formatting | bytes 1048576
where the time goes:
time: 120 us
  Pallas kernels  118 us (98%)
  local copies, waits for them, and re-layouts  1.87 us (2%)
    pallas_call x1, Pallas kernels, body(): pl.pallas_call(functools.partial(kernel, n_genome, n_samp, nb, half, trai...  118 us

commit v1 on v0

--- a/solution.py
+++ b/solution.py
@@ -12,6 +12,7 @@
 F32 = jnp.float32
 BF16 = jnp.bfloat16
 CONTRACT0 = (((0,), (0,)), ((), ()))
+PARTS = (2, 4, 8, 8)
 
 
 def gram(left, right):
@@ -21,7 +22,7 @@
 def kernel(
     n_genome, n_samp, nb, half, traits, scale,
     x_ref, e_ref, depth_ref, out_ref,
-    d_ref, own, xbuf, zbuf, eff, dep, loc, cro, par, far, lc_in, ly_out, ly_in, c_in, y_out, y_in, hop_out, hop_in,
+    d_ref, own, xbuf, zbuf, gacc, eff, dep, loc, cro, par, far, lc_in, ly_out, ly_in, c_in, y_out, y_in, hop_out, hop_in,
     own_sem, own_e_sem, x_send, x_recv, z_send, z_recv, es_send, es_recv, ex_send, ex_recv,
     ds_send, ds_recv, lc_send, lc_recv, ly_send, ly_recv, c_send, c_recv, y_send, y_recv, h_send, h_recv,
 ):
@@ -50,7 +51,6 @@
 
     my_cols = cols(s)
     keep_rows = pl.ds(pl.multiple_of(q * half, half), half)
-    give_rows = pl.ds(pl.multiple_of((1 - q) * half, half), half)
 
     def remote(src, dst, ss, rsem, gg, sss):
         return pltpu.make_async_remote_copy(
@@ -89,29 +89,46 @@
     def block_cols(b):
         return pl.ds(pl.multiple_of(b * BLK, BLK), BLK)
 
-    x_copies = [
-        remote(x_ref.at[give_rows, block_cols(other(t))], xbuf.at[t], x_send.at[t], x_recv.at[t], partner, s)
-        for t in range(nb)
-    ]
-    z_copies = [
-        remote(x_ref.at[keep_rows, block_cols(mine(t))], zbuf.at[t], z_send.at[t], z_recv.at[t], z_to, s)
-        for t in range(nb)
-    ]
+    last = nb - 1
+    pieces = []
+    for part in PARTS:
+        low = pieces[-1][1] if pieces else 0
+        pieces.append((low, low + half // part))
+
+    def half_rows(which, low, high):
+        return pl.ds(pl.multiple_of(which * half + low, 16), high - low)
+
+    def x_part(t, low, high, n):
+        return remote(
+            x_ref.at[half_rows(1 - q, low, high), block_cols(other(t))], xbuf.at[t, low:high],
+            x_send.at[n], x_recv.at[n], partner, s,
+        )
+
+    def z_part(t, low, high, n):
+        return remote(
+            x_ref.at[half_rows(q, low, high), block_cols(mine(t))], zbuf.at[t, low:high],
+            z_send.at[n], z_recv.at[n], z_to, s,
+        )
+
+    x_copies = [x_part(t, 0, half, t) for t in range(last)]
+    z_copies = [z_part(t, 0, half, t) for t in range(last)]
+    x_last = [x_part(last, low, high, last + n) for n, (low, high) in enumerate(pieces)]
+    z_last = [z_part(last, low, high, last + n) for n, (low, high) in enumerate(pieces)]
     d_x = remote(d_ref, dep.at[0], ds_send.at[0], ds_recv.at[0], partner, s)
     d_z = remote(d_ref, dep.at[1], ds_send.at[1], ds_recv.at[1], z_to, s)
     e_x = remote(e_ref, eff.at[1, :, my_cols], ex_send.at[0], ex_recv.at[0], partner, s)
     e_z = remote(e_ref, eff.at[2, :, my_cols], ex_send.at[1], ex_recv.at[1], z_to, s)
     d_x.start()
     e_x.start()
-    x_copies[0].start()
-    x_copies[1].start()
+    for c in x_copies + x_last:
+        c.start()
 
     @pl.when(has_to)
     def _():
         d_z.start()
         e_z.start()
-        z_copies[0].start()
-        z_copies[1].start()
+        for c in z_copies + z_last:
+            c.start()
 
     def gather(slot, source):
         across = cols(cross_mate)
@@ -257,99 +274,106 @@
         prepare(n, t)
         hop(n, t).start()
 
-    for t in range(nb):
+    def x_weight(t, u):
+        mu, mt = mine(u), mine(t)
+        drow = jnp.where(q == 0, d_ref[pl.ds(mu, 1), :], dep[0, pl.ds(mt, 1), :])
+        return weight(drow, jnp.int32(nb) + t - u)
+
+    def x_apply(t, u, full):
+        high = full.astype(BF16)
+        cro[rows(u), :] += jnp.dot(high, eff[1, rows(other(nb - 1 - t)), :], preferred_element_type=F32)
+        par[t * BLK : (t + 1) * BLK, :] += gram(high, eff[0, rows(mine(u)), :])
+
+    def z_weight(t, v):
+        mt, mv = mine(t), mine(v)
+        drow = jnp.where(q == 0, dep[0, pl.ds(mt, 1), :], dep[1, pl.ds(mv, 1), :])
+        return weight(drow, jnp.int32(nb) + v - t)
+
+    def z_apply(t, v, full):
+        high = full.astype(BF16)
+        par[t * BLK : (t + 1) * BLK, :] += jnp.dot(high, eff[2, rows(mine(v)), :], preferred_element_type=F32)
+        far[rows(v), :] += gram(high, eff[1, rows(mine(t)), :])
+
+    for t in range(last):
         x_copies[t].wait_recv()
-        if t == nb - 1:
-            for j in range(nb - 2):
-                hop(0, j).start()
-        if t + 2 < nb:
-            x_copies[t].wait_send()
-            x_copies[t + 2].start()
-
-            @pl.when(has_to)
-            def _():
-                z_copies[t].wait_send()
-                z_copies[t + 2].start()
 
         def x_pair(u, carry):
-            k = nb + t - u
-            mu, mt = mine(u), mine(t)
-            drow = jnp.where(q == 0, d_ref[pl.ds(mu, 1), :], dep[0, pl.ds(mt, 1), :])
-            full = gram(own[mu, keep_rows, :], xbuf[t]) * weight(drow, k)
-            high = full.astype(BF16)
-            cro[rows(u), :] += jnp.dot(high, eff[1, rows(other(nb - 1 - t)), :], preferred_element_type=F32)
-            par[t * BLK : (t + 1) * BLK, :] += gram(high, eff[0, rows(mu), :])
+            x_apply(t, u, gram(own[mine(u), keep_rows, :], xbuf[t]) * x_weight(t, u))
             return carry
-
-        if t > 0:
-            relay("partner", t - 1)
-            relay("own", t - 1)
-
-        if t == nb - 1:
-            x_pair(jnp.int32(t), 0)
-            publish("own", t)
 
         @pl.when(has_from)
         def _():
-            if t < nb - 1:
-                z_copies[t].wait_recv()
+            z_copies[t].wait_recv()
 
             def z_pair(v, carry):
-                k = nb + v - t
-                mt, mv = mine(t), mine(v)
-                drow = jnp.where(q == 0, dep[0, pl.ds(mt, 1), :], dep[1, pl.ds(mv, 1), :])
-                full = gram(xbuf[t], zbuf[v]) * weight(drow, jnp.int32(0) + k)
-                high = full.astype(BF16)
-                par[t * BLK : (t + 1) * BLK, :] += jnp.dot(high, eff[2, rows(mv), :], preferred_element_type=F32)
-                far[rows(v), :] += gram(high, eff[1, rows(mt), :])
+                z_apply(t, v, gram(xbuf[t], zbuf[v]) * z_weight(t, v))
                 return carry
 
-            if t < nb - 1:
-                lax.fori_loop(0, t + 1, z_pair, 0)
-            else:
-                for v in range(nb):
-                    if v == t:
-                        z_copies[t].wait_recv()
-                    z_pair(jnp.int32(v), 0)
+            lax.fori_loop(0, t + 1, z_pair, 0)
+
+        lax.fori_loop(t, nb, x_pair, 0)
+        publish("partner", t)
+        publish("own", t)
+        if t == 0:
+            loc_across.wait_recv()
+            out_ref[...] = loc[:, my_cols] + lc_in[my_y] + ly_in[...]
+        relay("partner", t)
+        relay("own", t)
+        prepare(0, t)
+        out_ref[rows(mine(t)), :] += collect("own", t)
+
+    for n, (low, high) in enumerate(pieces):
+        final = n == len(pieces) - 1
+        x_last[n].wait_recv()
+        if final:
+            for t in range(last):
+                hop(0, t).start()
+        mu = mine(jnp.int32(last))
+        x_piece = xbuf[last, low:high]
+        full = gram(own[mu, half_rows(q, low, high), :], x_piece)
+        if n:
+            full = gacc[nb] + full
+        if final:
+            x_apply(last, jnp.int32(last), full * x_weight(last, jnp.int32(last)))
+        else:
+            gacc[nb] = full
+
+        @pl.when(has_from)
+        def _():
+            for v in range(nb):
+                if v == last:
+                    z_last[n].wait_recv()
+                full = gram(xbuf[last, low:high], zbuf[v, low:high])
+                if n:
+                    full = gacc[v] + full
+                if final:
+                    z_apply(last, jnp.int32(v), full * z_weight(last, jnp.int32(v)))
                     publish("far", v)
                     if v > 0:
                         relay("far", v - 1)
-
-        if t < nb - 1:
-            lax.fori_loop(t, nb, x_pair, 0)
-        publish("partner", t)
-        if t < nb - 1:
-            publish("own", t)
-        if 0 < t < nb - 1:
-            prepare(0, t - 1)
-
-    @pl.when(has_from)
-    def _():
-        relay("far", nb - 1)
-
-    relay("partner", nb - 1)
-    relay("own", nb - 1)
-    forward(0, nb - 2)
-
-    @pl.when(has_from)
-    def _():
-        for v in range(nb - 1):
+                else:
+                    gacc[v] = full
+
+    publish("partner", last)
+    publish("own", last)
+
+    @pl.when(has_from)
+    def _():
+        relay("far", last)
+
+    relay("partner", last)
+    relay("own", last)
+
+    @pl.when(has_from)
+    def _():
+        for v in range(nb):
             forward(1, v)
 
-    loc_across.wait_recv()
-    out_ref[...] = loc[:, my_cols] + lc_in[my_y] + ly_in[...]
-    for t in range(nb - 1):
-        out_ref[rows(mine(t)), :] += collect("own", t)
-
-    @pl.when(has_from)
-    def _():
-        forward(1, nb - 1)
-
-    forward(0, nb - 1)
-    out_ref[rows(mine(nb - 1)), :] += collect("own", nb - 1)
-    for t in range(nb):
+    forward(0, last)
+    for t in range(last):
         hop(0, t).wait_recv()
         out_ref[rows(other(t)), :] += hop_in[0, t].astype(F32)
+    out_ref[rows(mine(last)), :] += collect("own", last)
 
     @pl.when(has_to)
     def _():
@@ -357,17 +381,20 @@
             hop(1, v).wait_recv()
             out_ref[rows(mine(v)), :] += hop_in[1, v].astype(F32)
 
+    hop(0, last).wait_recv()
+    out_ref[rows(other(last)), :] += hop_in[0, last].astype(F32)
+
     d_x.wait_send()
     e_x.wait_send()
-    for t in range(nb - 2, nb):
-        x_copies[t].wait_send()
+    for c in x_copies + x_last:
+        c.wait_send()
 
     @pl.when(has_to)
     def _():
         d_z.wait_send()
         e_z.wait_send()
-        for t in range(nb - 2, nb):
-            z_copies[t].wait_send()
+        for c in z_copies + z_last:
+            c.wait_send()
 
     for c in e_own + e_partner + [loc_core(0), loc_core(1), loc_across]:
         c.wait_send()
@@ -408,6 +435,7 @@
             pltpu.VMEM((nb, samples, BLK), BF16),
             pltpu.VMEM((nb, half, BLK), BF16),
             pltpu.VMEM((nb, half, BLK), BF16),
+            pltpu.VMEM((nb + 1, BLK, BLK), F32),
             pltpu.VMEM((3, variants, all_traits), BF16),
             pltpu.VMEM((2, 8, BLK), F32),
             pltpu.VMEM((variants, all_traits), F32),
@@ -423,7 +451,8 @@
             pltpu.VMEM((2, nb, BLK, traits), BF16),
             pltpu.VMEM((2, nb, BLK, traits), BF16),
             dma((nb,)), dma((1,)),
-            dma((nb,)), dma((nb,)), dma((nb,)), dma((nb,)),
+            dma((nb - 1 + len(PARTS),)), dma((nb - 1 + len(PARTS),)),
+            dma((nb - 1 + len(PARTS),)), dma((nb - 1 + len(PARTS),)),
             dma((3, 3)), dma((3, 3)),
             dma((2,)), dma((2,)), dma((2,)), dma((2,)),
             dma((2,)), dma((2,)), dma((1,)), dma((1,)),

time: 120 us -> 119 us (level)
  no operation moved by 1% of the time
where the time goes in v1:
time: 119 us
  Pallas kernels  117 us (98%)
  local copies, waits for them, and re-layouts  1.87 us (2%)
    pallas_call x1, Pallas kernels, body(): pl.pallas_call(functools.partial(kernel, n_genome, n_samp, nb, half, trai...  117 us

profile of v1, /device:TPU:0, one launch (start us, length us, event | category | flops | bytes accessed | tf_op | source)
XLA Modules:
  0.0 119.2 jit_solution(17483335049848628991)
XLA Ops:
  0.0 117.3 %shard_map.37 = f32[1024,128]{1,0:T(8,128)} custom-call(bf16[4096,1024]{1,0:T(8,128)(2,1)} %x_ref.1, bf16[1024,128]{1,0:T(8,128)(2,1)} %e_ref.1, s32[4]{0:T(128)} %depth_ref.1), custom_call_target="tpu_custom_call" | custom-call | flops 10737418240 | bytes 16777216 | tf_op jit(solution)/shard_map/pallas_call | solution.py:424
  117.3 1.9 %copy.5 = f32[1024,128]{1,0:T(8,128)} copy(f32[1024,128]{1,0:T(8,128)} %shard_map.37) | data formatting | bytes 1048576

commit v2 on v1

--- a/solution.py
+++ b/solution.py
@@ -423,7 +423,7 @@
     dma = pltpu.SemaphoreType.DMA
     return pl.pallas_call(
         functools.partial(kernel, n_genome, n_samp, nb, half, traits, 1.0 / (samples * n_samp)),
-        out_shape=jax.ShapeDtypeStruct((variants, traits), F32),
+        out_shape=pltpu.VMEM((variants, traits), F32),
         in_specs=[
             pl.BlockSpec(memory_space=pl.ANY),
             pl.BlockSpec(memory_space=pl.ANY),

time: 119 us -> 117 us (0.983)
  no operation moved by 1% of the time
where the time goes in v2:
time: 117 us
  Pallas kernels  117 us (100%)
    pallas_call x1, Pallas kernels, body(): pl.pallas_call(functools.partial(kernel, n_genome, n_samp, nb, half, trai...  117 us

profile of v2, /device:TPU:0, one launch (start us, length us, event | category | flops | bytes accessed | tf_op | source)
XLA Modules:
  0.0 117.3 jit_solution(5243331310326818385)
XLA Ops:
  0.0 116.5 %shard_map.37 = f32[1024,128]{1,0:T(8,128)S(1)} custom-call(bf16[4096,1024]{1,0:T(8,128)(2,1)} %x_ref.1, bf16[1024,128]{1,0:T(8,128)(2,1)} %e_ref.1, s32[4]{0:T(128)} %depth_ref.1), custom_call_target="tpu_custom_call" | custom-call | flops 10737418240 | bytes 16777216 | tf_op jit(solution)/shard_map/pallas_call | solution.py:424
  116.5 0.8 copy.5

commit v3 on v2

v3 whole, which is shorter than its diff:
```python
import functools

import jax
import jax.numpy as jnp
from jax import lax
from jax.experimental import pallas as pl
from jax.experimental.pallas import tpu as pltpu
from jax.sharding import PartitionSpec as P

BLK = 256
HB = BLK // 2
MESH = pl.DeviceIdType.MESH
F32 = jnp.float32
BF16 = jnp.bfloat16
CONTRACT0 = (((0,), (0,)), ((), ()))
PARTS = (2, 4, 8, 8)


def gram(left, right):
    return lax.dot_general(left, right, CONTRACT0, preferred_element_type=F32)


def dot(left, right):
    return jnp.dot(left, right, preferred_element_type=F32)


def make_groups(nb):
    last = nb - 1
    split = last * BLK + HB
    x = [(t, nb, t * BLK, (t + 1) * BLK) for t in range(last)]
    x += [(last, nb, last * BLK, split), (last, nb, split, nb * BLK)]
    z = [(0, t + 1, t * BLK, (t + 1) * BLK) for t in range(last)]
    z += [(0, last, last * BLK, split)]
    z += [(v, v + 1, split, nb * BLK) for v in range(last)] + [(last, nb, last * BLK, nb * BLK)]
    return x, z


def kernel(
    n_genome, n_samp, nb, half, scale,
    x_ref, e_ref, depth_ref, out_ref,
    d_ref, dep, own, xbuf, zbuf, eff,
    sum_x, sum_z, sum_l, cin_x, cin_z, cin_l, yo_x, yo_z, yo_l, yi_x, yi_z, yi_l, cor_x, cor_z, cor_l,
    acc, par, far, hop_out, hop_in,
    own_sem, own_e_sem, x_send, x_recv, z_send, z_recv, ex_send, ex_recv, ez_send, ez_recv, ds_send, ds_recv,
    a_send, a_recv, b_send, b_recv, c_send, c_recv, h_send, h_recv,
):
    g = lax.axis_index("genome")
    s = lax.axis_index("samp")
    q = lax.rem(g, 2)
    sign = 1 - 2 * q
    partner = g + sign
    z_from = g + 2 * sign
    z_to = g - 2 * sign
    has_from = jnp.logical_and(z_from >= 0, z_from < n_genome)
    has_to = jnp.logical_and(z_to >= 0, z_to < n_genome)
    last = nb - 1
    split = last * BLK + HB

    def mine(u):
        return u + q * (nb - 1 - 2 * u)

    def other(u):
        return nb - 1 - mine(u)

    core = lax.rem(s, 2)
    core_mate = s + 1 - 2 * core
    cross_mate = lax.rem(s + 2, n_samp)

    def remote(src, dst, ss, rsem, gg, sss):
        return pltpu.make_async_remote_copy(
            src_ref=src, dst_ref=dst, send_sem=ss, recv_sem=rsem,
            device_id=(gg, sss), device_id_type=MESH,
        )

    def at_block(b):
        return pl.ds(pl.multiple_of(b * BLK, BLK), BLK)

    def half_rows(which, low, high):
        return pl.ds(pl.multiple_of(which * half + low, 16), high - low)

    barrier = pltpu.get_barrier_semaphore()
    for mate in (core_mate, cross_mate):
        pl.semaphore_signal(barrier, inc=1, device_id=(g, mate), device_id_type=MESH)
    pl.semaphore_signal(barrier, inc=1, device_id=(partner, s), device_id_type=MESH)

    @pl.when(has_from)
    def _():
        pl.semaphore_signal(barrier, inc=1, device_id=(z_from, s), device_id_type=MESH)

    @pl.when(has_to)
    def _():
        pl.semaphore_signal(barrier, inc=1, device_id=(z_to, s), device_id_type=MESH)

    own_copies = [
        pltpu.make_async_copy(x_ref.at[:, at_block(mine(u))], own.at[u], own_sem.at[u]) for u in range(nb)
    ]
    own_effects = [
        pltpu.make_async_copy(e_ref.at[at_block(mine(u)), :], eff.at[0, u * BLK : (u + 1) * BLK], own_e_sem.at[u])
        for u in range(nb)
    ]
    for c in own_copies + own_effects:
        c.start()
    for u in range(nb):
        d_ref[u : u + 1, :] = jnp.full((1, BLK), depth_ref[mine(u)].astype(F32))
    pl.semaphore_wait(
        barrier, 3 + has_from.astype(jnp.int32) + has_to.astype(jnp.int32)
    )

    pieces = []
    for part in PARTS:
        low = pieces[-1][1] if pieces else 0
        pieces.append((low, low + half // part))

    def x_part(t, low, high, left, right, n):
        src = pl.ds(pl.multiple_of(other(t) * BLK + left, HB), right - left)
        return remote(
            x_ref.at[half_rows(1 - q, low, high), src], xbuf.at[t, low:high, left:right],
            x_send.at[n], x_recv.at[n], partner, s,
        )

    def z_part(t, low, high, n):
        return remote(
            x_ref.at[half_rows(q, low, high), at_block(mine(t))], zbuf.at[t, low:high],
            z_send.at[n], z_recv.at[n], z_to, s,
        )

    x_copies = [x_part(t, 0, half, 0, BLK, t) for t in range(last)] + [x_part(last, 0, half, 0, HB, last)]
    z_copies = [z_part(t, 0, half, t) for t in range(last)]
    x_last = [x_part(last, low, high, HB, BLK, nb + n) for n, (low, high) in enumerate(pieces)]
    z_last = [z_part(last, low, high, last + n) for n, (low, high) in enumerate(pieces)]
    e_x = [
        remote(e_ref.at[at_block(other(t)), :], eff.at[1, t * BLK : (t + 1) * BLK], ex_send.at[t], ex_recv.at[t], partner, s)
        for t in range(nb)
    ]
    e_z = [
        remote(e_ref.at[at_block(mine(v)), :], eff.at[2, v * BLK : (v + 1) * BLK], ez_send.at[v], ez_recv.at[v], z_to, s)
        for v in range(nb)
    ]
    d_x = remote(d_ref, dep.at[0], ds_send.at[0], ds_recv.at[0], partner, s)
    d_z = remote(d_ref, dep.at[1], ds_send.at[1], ds_recv.at[1], z_to, s)
    to_partner = [d_x] + x_copies + x_last + e_x
    to_next = [d_z] + z_copies + z_last + e_z
    for c in to_partner:
        c.start()

    @pl.when(has_to)
    def _():
        for c in to_next:
            c.start()

    groups_x, groups_z = make_groups(nb)
    n_x = len(groups_x)
    refs_x = (sum_x, cin_x, yo_x, yi_x, cor_x)
    refs_z = (sum_z, cin_z, yo_z, yi_z, cor_z)
    refs_l = (sum_l, cin_l, yo_l, yi_l, cor_l)
    X = [(i, refs_x) + gr for i, gr in enumerate(groups_x)]
    Z = [(n_x + i, refs_z) + gr for i, gr in enumerate(groups_z)]
    L = (n_x + len(groups_z), refs_l, 0, nb * (nb + 1) // 2, 0, BLK)

    def to_core(group):
        i, (total, cin, _, _, _), low, high, left, right = group
        return remote(
            total.at[low:high, 1 - core, :, left:right], cin.at[low:high, :, left:right],
            a_send.at[i], a_recv.at[i], g, core_mate,
        )

    def to_cross(group):
        i, (_, _, y_out, y_in, _), low, high, left, right = group
        return remote(
            y_out.at[low:high, :, left:right], y_in.at[low:high, :, left:right],
            b_send.at[i], b_recv.at[i], g, cross_mate,
        )

    def share(group):
        i, (_, _, _, _, corr), low, high, left, right = group
        part = corr.at[low:high, core, :, left:right]
        return remote(part, part, c_send.at[i], c_recv.at[i], g, core_mate)

    def stage1(group):
        to_core(group).start()

    def stage2(group):
        i, (total, cin, y_out, _, _), low, high, left, right = group
        to_core(group).wait_recv()
        for a in range(low, high):
            value = total[a, core, :, left:right] + cin[a, :, left:right]
            total[a, core, :, left:right] = value
            y_out[a, :, left:right] = value.astype(y_out.dtype)
        to_cross(group).start()

    def stage3(group):
        i, (total, _, _, y_in, corr), low, high, left, right = group
        to_cross(group).wait_recv()
        for a in range(low, high):
            value = total[a, core, :, left:right] + y_in[a, :, left:right].astype(F32)
            corr[a, core, :, left:right] = value.astype(BF16)
        share(group).start()

    def stage4(group):
        share(group).wait_recv()

    def weight(drow, k, width):
        return jnp.where(drow >= jnp.asarray(k, F32), F32(scale), F32(0.0))[:, :width]

    def row_of(ref, n):
        return ref[pl.ds(n, 1), :]

    def x_weight(t, u, width):
        drow = jnp.where(q == 0, row_of(d_ref, u), row_of(dep.at[0], nb - 1 - t))
        return weight(drow, (nb + t - u), width)

    def z_weight(t, v, width):
        drow = jnp.where(q == 0, row_of(dep.at[0], nb - 1 - t), row_of(dep.at[1], v))
        return weight(drow, (nb + v - t), width)

    def put(ref, a, left, right, value):
        for h in range(2):
            ref[a, h, :, left:right] = value[h * HB : (h + 1) * HB]

    def got(ref, a, left, right):
        return ref[a, :, :, left:right].reshape(BLK, right - left)

    def stack(ref, low, high, left, right):
        return ref[low:high, :, :, left:right].reshape((high - low) * BLK, right - left)

    def block(n):
        return slice(n * BLK, (n + 1) * BLK)

    for c in own_copies + own_effects:
        c.wait()

    def local_row(i, carry):
        def local_pair(j, carry):
            full = gram(own[i, :half], own[j, :half]) + gram(own[i, half:], own[j, half:])
            drow = jnp.where(q == 0, row_of(d_ref, i), row_of(d_ref, j))
            full = full * weight(drow, (j - i).astype(F32), BLK)
            put(sum_l, i * (2 * nb - i + 1) // 2 + (j - i), 0, BLK, full)
            return carry

        return lax.fori_loop(i, nb, local_pair, carry)

    lax.fori_loop(0, nb, local_row, 0)
    stage1(L)
    acc[...] = jnp.zeros_like(acc)
    stage2(L)
    d_x.wait_recv()

    @pl.when(has_from)
    def _():
        d_z.wait_recv()

    def x_grams(t, left, right):
        def pair(u, carry):
            full = gram(own[u, half_rows(q, 0, half), :], xbuf[t, :, left:right])
            put(sum_x, u, t * BLK + left, t * BLK + right, full * x_weight(t, u, right - left))
            return carry

        lax.fori_loop(t, nb, pair, 0)

    def z_grams(t, left, right, count):
        def pair(v, carry):
            full = gram(zbuf[v], xbuf[t, :, left:right])
            put(sum_z, v, t * BLK + left, t * BLK + right, full * z_weight(t, v, right - left))
            return carry

        lax.fori_loop(0, count, pair, 0)

    def local_products():
        def local_row(i, carry):
            def local_pair(j, carry):
                corr = got(cor_l, i * (2 * nb - i + 1) // 2 + (j - i), 0, BLK)
                acc[at_block(i), :] += dot(corr, eff[0, at_block(j), :])

                @pl.when(j > i)
                def _():
                    acc[at_block(j), :] += gram(corr, eff[0, at_block(i), :])

                return carry

            return lax.fori_loop(i, nb, local_pair, carry)

        lax.fori_loop(0, nb, local_row, 0)

    def both(stage, t):
        stage(X[t])

        @pl.when(has_from)
        def _():
            stage(Z[t])

    for t in range(nb):
        left, right = (0, BLK) if t < last else (0, HB)
        x_copies[t].wait_recv()
        x_grams(t, left, right)
        stage1(X[t])

        @pl.when(has_from)
        def _():
            if t < last:
                z_copies[t].wait_recv()
            z_grams(t, left, right, min(t + 1, last))
            stage1(Z[t])

        both(stage2, t)
        if t == 1:
            stage3(L)
            both(stage3, 0)
            stage4(L)
            local_products()
            both(stage4, 0)
        if t == 2:
            both(stage3, 1)
            both(stage4, 1)

    late_x = X[nb]
    late_z = Z[nb:]
    for n, (low, high) in enumerate(pieces):
        final = n == len(pieces) - 1

        def add(ref, a, left, right, value, factor):
            for h in range(2):
                part = value[h * HB : (h + 1) * HB]
                if n:
                    part = ref[a, h, :, left:right] + part
                ref[a, h, :, left:right] = part * factor if final else part

        if n == 1:
            both(stage3, 2)
        x_last[n].wait_recv()

        @pl.when(has_from)
        def _():
            for v in range(nb):
                if v == last:
                    z_last[n].wait_recv()
                left = HB if v < last else 0
                full = gram(zbuf[v, low:high], xbuf[last, low:high, left:])
                add(sum_z, v, last * BLK + left, nb * BLK, full, z_weight(last, v, BLK - left) if final else None)
                if final:
                    stage1(late_z[v])

        full = gram(own[last, half_rows(q, low, high), :], xbuf[last, low:high, HB:])
        add(sum_x, last, split, nb * BLK, full, x_weight(last, last, HB) if final else None)
        if final:
            stage1(late_x)

    @pl.when(has_from)
    def _():
        for v in range(nb):
            stage2(late_z[v])

    stage2(late_x)
    both(stage4, 2)
    both(stage3, last)

    def hop(n, t):
        return remote(
            hop_out.at[n, t], hop_in.at[n, t], h_send.at[n, t], h_recv.at[n, t],
            partner if n == 0 else z_from, s,
        )

    for t in range(last):
        par[block(t), :] = gram(stack(cor_x, t, nb, t * BLK, (t + 1) * BLK), eff[0, t * BLK :])
    both(stage4, last)
    par[last * BLK : split, :] = gram(got(cor_x, last, last * BLK, split), eff[0, block(last)])

    @pl.when(has_from)
    def _():
        for c in e_z:
            c.wait_recv()
        for t in range(last):
            par[block(t), :] += gram(stack(cor_z, 0, t + 1, t * BLK, (t + 1) * BLK), eff[2, : (t + 1) * BLK])

    for t in range(last):
        hop_out[0, t] = par[block(t), :].astype(BF16)
        hop(0, t).start()

    @pl.when(has_from)
    def _():
        stage3(late_z[0])
        stage3(late_z[1])
        par[last * BLK : split, :] += gram(stack(cor_z, 0, last, last * BLK, split), eff[2, : last * BLK])

    for c in e_x:
        c.wait_recv()

    @pl.when(has_from)
    def _():
        for v in range(last):
            far[block(v), :] = dot(got(cor_z, v, v * BLK, split), eff[1, v * BLK : split])
        for v in range(2, nb):
            stage3(late_z[v])

    stage3(late_x)

    @pl.when(has_from)
    def _():
        for v in range(nb):
            stage4(late_z[v])
            if v < last:
                hop_out[1, v] = (far[block(v), :] + dot(got(cor_z, v, split, nb * BLK), eff[1, split:])).astype(BF16)
            else:
                hop_out[1, v] = dot(got(cor_z, v, last * BLK, nb * BLK), eff[1, last * BLK :]).astype(BF16)
            hop(1, v).start()

    stage4(late_x)
    par[split:, :] = gram(got(cor_x, last, split, nb * BLK), eff[0, block(last)])

    @pl.when(has_from)
    def _():
        par[split:, :] += gram(stack(cor_z, 0, last, split, nb * BLK), eff[2, : last * BLK])
        par[block(last), :] += gram(got(cor_z, last, last * BLK, nb * BLK), eff[2, block(last)])

    hop_out[0, last] = par[block(last), :].astype(BF16)
    hop(0, last).start()
    for u in range(nb):
        acc[block(u), :] += dot(got(cor_x, u, 0, (u + 1) * BLK), eff[1, : (u + 1) * BLK])
    for u in range(nb - 1, -1, -1):
        hop(0, nb - 1 - u).wait_recv()
        out_ref[at_block(mine(u)), :] = acc[block(u), :] + hop_in[0, nb - 1 - u].astype(F32)

    @pl.when(has_to)
    def _():
        for v in range(nb):
            hop(1, v).wait_recv()
            out_ref[at_block(mine(v)), :] += hop_in[1, v].astype(F32)

    for c in to_partner:
        c.wait_send()

    @pl.when(has_to)
    def _():
        for c in to_next:
            c.wait_send()

    for group in X + [L]:
        for c in (to_core(group), to_cross(group), share(group)):
            c.wait_send()
    for t in range(nb):
        hop(0, t).wait_send()

    @pl.when(has_from)
    def _():
        for group in Z:
            for c in (to_core(group), to_cross(group), share(group)):
                c.wait_send()
        for t in range(nb):
            hop(1, t).wait_send()


def body(n_genome, n_samp, dosage, effects, depth):
    nb = depth.shape[0]
    samples, variants = dosage.shape
    traits = effects.shape[1]
    half = samples // 2
    dma = pltpu.SemaphoreType.DMA
    pairs = nb * (nb + 1) // 2
    groups_x, groups_z = make_groups(nb)
    n_groups = len(groups_x) + len(groups_z) + 1

    def pair_of(kind, lead, dtype, lead_l=()):
        wide = pltpu.VMEM((nb,) + lead + (HB, variants), dtype)
        return [wide, wide, pltpu.VMEM((pairs,) + lead + (HB, BLK), kind)]

    return pl.pallas_call(
        functools.partial(kernel, n_genome, n_samp, nb, half, 1.0 / (samples * n_samp)),
        out_shape=pltpu.VMEM((variants, traits), F32),
        in_specs=[
            pl.BlockSpec(memory_space=pl.ANY),
            pl.BlockSpec(memory_space=pl.ANY),
            pl.BlockSpec(memory_space=pltpu.SMEM),
        ],
        out_specs=pl.BlockSpec(memory_space=pltpu.VMEM),
        scratch_shapes=[
            pltpu.VMEM((8, BLK), F32),
            pltpu.VMEM((2, 8, BLK), F32),
            pltpu.VMEM((nb, samples, BLK), BF16),
            pltpu.VMEM((nb, half, BLK), BF16),
            pltpu.VMEM((nb, half, BLK), BF16),
            pltpu.VMEM((3, variants, traits), BF16),
            *pair_of(F32, (2,), F32),
            *pair_of(F32, (), F32),
            *pair_of(F32, (), BF16),
            *pair_of(F32, (), BF16),
            *pair_of(BF16, (2,), BF16),
            pltpu.VMEM((variants, traits), F32),
            pltpu.VMEM((variants, traits), F32),
            pltpu.VMEM((variants, traits), F32),
            pltpu.VMEM((2, nb, BLK, traits), BF16),
            pltpu.VMEM((2, nb, BLK, traits), BF16),
            dma((nb,)), dma((nb,)),
            dma((nb + len(PARTS),)), dma((nb + len(PARTS),)),
            dma((nb + len(PARTS),)), dma((nb + len(PARTS),)),
            dma((nb,)), dma((nb,)), dma((nb,)), dma((nb,)), dma((2,)), dma((2,)),
            dma((n_groups,)), dma((n_groups,)), dma((n_groups,)), dma((n_groups,)), dma((n_groups,)), dma((n_groups,)),
            dma((2, nb)), dma((2, nb)),
        ],
        compiler_params=pltpu.CompilerParams(
            collective_id=0, has_side_effects=True, vmem_limit_bytes=60 * 1024 * 1024
        ),
        cost_estimate=pl.CostEstimate(
            flops=2 * 20 * BLK * BLK * samples, bytes_accessed=4 * samples * variants, transcendentals=0
        ),
    )(dosage, effects, depth)


def solution(mesh):
    return jax.shard_map(
        functools.partial(body, mesh.shape["genome"], mesh.shape["samp"]),
        mesh=mesh,
        in_specs=(P("samp", "genome"), P("genome", "samp"), P("genome")),
        out_specs=P("genome", "samp"),
        check_vma=False,
    )
```

time: 117 us -> 113 us (0.966)
  Pallas kernels: 117 us -> 112 us
    pallas_call x1, Pallas kernels: 117 us -> 112 us  [body(): pl.pallas_call(functools.partial(kernel, n_genome, n_samp, nb, half, 1.0...]
where the time goes in v3:
time: 113 us
  Pallas kernels  112 us (99%)
    pallas_call x1, Pallas kernels, body(): pl.pallas_call(functools.partial(kernel, n_genome, n_samp, nb, half, 1.0...  112 us

profile of v3, /device:TPU:0, one launch (start us, length us, event | category | flops | bytes accessed | tf_op | source)
XLA Modules:
  0.0 113.2 jit_solution(5746054141624733792)
XLA Ops:
  0.0 112.4 %shard_map.37 = f32[1024,128]{1,0:T(8,128)S(1)} custom-call(bf16[4096,1024]{1,0:T(8,128)(2,1)} %x_ref.1, bf16[1024,128]{1,0:T(8,128)(2,1)} %e_ref.1, s32[4]{0:T(128)} %depth_ref.1), custom_call_target="tpu_custom_call" | custom-call | flops 10737418240 | bytes 16777216 | tf_op jit(solution)/shard_map/pallas_call | solution.py:465
  112.4 0.8 copy.5

commit v4 on v3

--- a/solution.py
+++ b/solution.py
@@ -25,21 +25,23 @@
 
 
 def make_groups(nb):
-    last = nb - 1
-    split = last * BLK + HB
-    x = [(t, nb, t * BLK, (t + 1) * BLK) for t in range(last)]
-    x += [(last, nb, last * BLK, split), (last, nb, split, nb * BLK)]
-    z = [(0, t + 1, t * BLK, (t + 1) * BLK) for t in range(last)]
-    z += [(0, last, last * BLK, split)]
-    z += [(v, v + 1, split, nb * BLK) for v in range(last)] + [(last, nb, last * BLK, nb * BLK)]
-    return x, z
+    def cols(t):
+        return t * BLK, (t + 1) * BLK
+
+    x = [[(t, nb) + cols(t)] for t in range(1, nb)] + [[(0, nb, 0, HB)]]
+    x += [[(u, u + 2, HB, BLK) for u in range(0, nb, 2)]]
+    z = [[(0, t) + cols(t)] + ([(t - 1, t) + cols(t - 1)] if t > 1 else []) for t in range(1, nb)]
+    z += [[(0, 1, 0, HB)], [(0, 1, HB, BLK)]]
+    w = [[(0, 1, 0, HB)], [(0, 1, HB, BLK)]]
+    return x, z, w
 
 
 def kernel(
     n_genome, n_samp, nb, half, scale,
     x_ref, e_ref, depth_ref, out_ref,
     d_ref, dep, own, xbuf, zbuf, eff,
-    sum_x, sum_z, sum_l, cin_x, cin_z, cin_l, yo_x, yo_z, yo_l, yi_x, yi_z, yi_l, cor_x, cor_z, cor_l,
+    sum_x, sum_z, sum_w, sum_l, cin_x, cin_z, cin_w, cin_l, yo_x, yo_z, yo_w, yo_l, yi_x, yi_z, yi_w, yi_l,
+    cor_x, cor_z, cor_w, cor_l,
     acc, par, far, hop_out, hop_in,
     own_sem, own_e_sem, x_send, x_recv, z_send, z_recv, ex_send, ex_recv, ez_send, ez_recv, ds_send, ds_recv,
     a_send, a_recv, b_send, b_recv, c_send, c_recv, h_send, h_recv,
@@ -54,7 +56,6 @@
     has_from = jnp.logical_and(z_from >= 0, z_from < n_genome)
     has_to = jnp.logical_and(z_to >= 0, z_to < n_genome)
     last = nb - 1
-    split = last * BLK + HB
 
     def mine(u):
         return u + q * (nb - 1 - 2 * u)
@@ -118,16 +119,17 @@
             x_send.at[n], x_recv.at[n], partner, s,
         )
 
-    def z_part(t, low, high, n):
+    def z_part(v, low, high, left, right, n):
+        src = pl.ds(pl.multiple_of(mine(v) * BLK + left, HB), right - left)
         return remote(
-            x_ref.at[half_rows(q, low, high), at_block(mine(t))], zbuf.at[t, low:high],
+            x_ref.at[half_rows(q, low, high), src], zbuf.at[v, low:high, left:right],
             z_send.at[n], z_recv.at[n], z_to, s,
         )
 
-    x_copies = [x_part(t, 0, half, 0, BLK, t) for t in range(last)] + [x_part(last, 0, half, 0, HB, last)]
-    z_copies = [z_part(t, 0, half, t) for t in range(last)]
-    x_last = [x_part(last, low, high, HB, BLK, nb + n) for n, (low, high) in enumerate(pieces)]
-    z_last = [z_part(last, low, high, last + n) for n, (low, high) in enumerate(pieces)]
+    x_copies = [x_part(k + 1, 0, half, 0, BLK, k) for k in range(last)] + [x_part(0, 0, half, 0, HB, last)]
+    z_copies = [z_part(k, 0, half, 0, BLK, k) for k in range(last)] + [z_part(last, 0, half, 0, HB, last)]
+    x_last = [x_part(0, low, high, HB, BLK, nb + n) for n, (low, high) in enumerate(pieces)]
+    z_last = [z_part(last, low, high, HB, BLK, nb + n) for n, (low, high) in enumerate(pieces)]
     e_x = [
         remote(e_ref.at[at_block(other(t)), :], eff.at[1, t * BLK : (t + 1) * BLK], ex_send.at[t], ex_recv.at[t], partner, s)
         for t in range(nb)
@@ -138,7 +140,7 @@
     ]
     d_x = remote(d_ref, dep.at[0], ds_send.at[0], ds_recv.at[0], partner, s)
     d_z = remote(d_ref, dep.at[1], ds_send.at[1], ds_recv.at[1], z_to, s)
-    to_partner = [d_x] + x_copies + x_last + e_x
+    to_partner = [d_x] + x_copies + x_last + e_x[::-1]
     to_next = [d_z] + z_copies + z_last + e_z
     for c in to_partner:
         c.start()
@@ -148,14 +150,20 @@
         for c in to_next:
             c.start()
 
-    groups_x, groups_z = make_groups(nb)
-    n_x = len(groups_x)
-    refs_x = (sum_x, cin_x, yo_x, yi_x, cor_x)
-    refs_z = (sum_z, cin_z, yo_z, yi_z, cor_z)
-    refs_l = (sum_l, cin_l, yo_l, yi_l, cor_l)
-    X = [(i, refs_x) + gr for i, gr in enumerate(groups_x)]
-    Z = [(n_x + i, refs_z) + gr for i, gr in enumerate(groups_z)]
-    L = (n_x + len(groups_z), refs_l, 0, nb * (nb + 1) // 2, 0, BLK)
+    counter = [0]
+
+    def label(steps, refs):
+        out = []
+        for step in steps:
+            out.append([(counter[0] + n, refs) + gr for n, gr in enumerate(step)])
+            counter[0] += len(step)
+        return out
+
+    groups_x, groups_z, groups_w = make_groups(nb)
+    X = label(groups_x, (sum_x, cin_x, yo_x, yi_x, cor_x))
+    Z = label(groups_z, (sum_z, cin_z, yo_z, yi_z, cor_z))
+    W = label(groups_w, (sum_w, cin_w, yo_w, yi_w, cor_w))
+    L = label([[(0, nb * (nb + 1) // 2, 0, BLK)]], (sum_l, cin_l, yo_l, yi_l, cor_l))[0][0]
 
     def to_core(group):
         i, (total, cin, _, _, _), low, high, left, right = group
@@ -257,13 +265,13 @@
 
         lax.fori_loop(t, nb, pair, 0)
 
-    def z_grams(t, left, right, count):
+    def z_grams(low, high, t, left, right):
         def pair(v, carry):
             full = gram(zbuf[v], xbuf[t, :, left:right])
             put(sum_z, v, t * BLK + left, t * BLK + right, full * z_weight(t, v, right - left))
             return carry
 
-        lax.fori_loop(0, count, pair, 0)
+        lax.fori_loop(low, high, pair, 0)
 
     def local_products():
         def local_row(i, carry):
@@ -281,48 +289,59 @@
 
         lax.fori_loop(0, nb, local_row, 0)
 
-    def both(stage, t):
-        stage(X[t])
+    def from_groups(k):
+        return Z[k] + (W[k - last] if k >= last else [])
+
+    def both(stage, k):
+        for group in X[k]:
+            stage(group)
 
         @pl.when(has_from)
         def _():
-            stage(Z[t])
-
-    for t in range(nb):
-        left, right = (0, BLK) if t < last else (0, HB)
-        x_copies[t].wait_recv()
+            for group in from_groups(k):
+                stage(group)
+
+    for k in range(nb):
+        t, left, right = (k + 1, 0, BLK) if k < last else (0, 0, HB)
+        x_copies[k].wait_recv()
         x_grams(t, left, right)
-        stage1(X[t])
+        stage1(X[k][0])
 
         @pl.when(has_from)
         def _():
-            if t < last:
-                z_copies[t].wait_recv()
-            z_grams(t, left, right, min(t + 1, last))
-            stage1(Z[t])
-
-        both(stage2, t)
-        if t == 1:
+            z_copies[k].wait_recv()
+            if k < last:
+                z_grams(0, t, t, left, right)
+                if k:
+                    z_grams(k, k + 1, k, left, right)
+            else:
+                z_grams(0, 1, 0, left, right)
+                full = gram(xbuf[last], zbuf[last, :, left:right])
+                put(sum_w, 0, left, right, full * z_weight(last, last, HB))
+            for group in from_groups(k):
+                stage1(group)
+
+        both(stage2, k)
+        if k == 1:
             stage3(L)
             both(stage3, 0)
             stage4(L)
             local_products()
             both(stage4, 0)
-        if t == 2:
+        if k == 2:
             both(stage3, 1)
             both(stage4, 1)
 
-    late_x = X[nb]
-    late_z = Z[nb:]
+    late_z, late_w = Z[nb][0], W[1][0]
     for n, (low, high) in enumerate(pieces):
         final = n == len(pieces) - 1
 
-        def add(ref, a, left, right, value, factor):
+        def add(ref, a, value, factor):
             for h in range(2):
                 part = value[h * HB : (h + 1) * HB]
                 if n:
-                    part = ref[a, h, :, left:right] + part
-                ref[a, h, :, left:right] = part * factor if final else part
+                    part = ref[a, h, :, HB:BLK] + part
+                ref[a, h, :, HB:BLK] = part * factor if final else part
 
         if n == 1:
             both(stage3, 2)
@@ -330,100 +349,122 @@
 
         @pl.when(has_from)
         def _():
-            for v in range(nb):
-                if v == last:
-                    z_last[n].wait_recv()
-                left = HB if v < last else 0
-                full = gram(zbuf[v, low:high], xbuf[last, low:high, left:])
-                add(sum_z, v, last * BLK + left, nb * BLK, full, z_weight(last, v, BLK - left) if final else None)
-                if final:
-                    stage1(late_z[v])
-
-        full = gram(own[last, half_rows(q, low, high), :], xbuf[last, low:high, HB:])
-        add(sum_x, last, split, nb * BLK, full, x_weight(last, last, HB) if final else None)
-        if final:
-            stage1(late_x)
-
-    @pl.when(has_from)
-    def _():
-        for v in range(nb):
-            stage2(late_z[v])
-
-    stage2(late_x)
+            full = gram(zbuf[0, low:high], xbuf[0, low:high, HB:])
+            add(sum_z, 0, full, z_weight(0, 0, HB) if final else None)
+            if final:
+                stage1(late_z)
+            z_last[n].wait_recv()
+            full = gram(xbuf[last, low:high], zbuf[last, low:high, HB:])
+            add(sum_w, 0, full, z_weight(last, last, HB) if final else None)
+            if final:
+                stage1(late_w)
+
+        for u in range(nb):
+            full = gram(own[u, half_rows(q, low, high), :], xbuf[0, low:high, HB:])
+            add(sum_x, u, full, x_weight(0, u, HB) if final else None)
+            if final and u % 2:
+                stage1(X[nb][u // 2])
+
+    @pl.when(has_from)
+    def _():
+        stage2(late_z)
+        stage2(late_w)
+
+    for group in X[nb]:
+        stage2(group)
     both(stage4, 2)
     both(stage3, last)
 
-    def hop(n, t):
+    def hop(n, t, low=0, high=BLK):
+        i = nb if low else t
         return remote(
-            hop_out.at[n, t], hop_in.at[n, t], h_send.at[n, t], h_recv.at[n, t],
+            hop_out.at[n, t, low:high], hop_in.at[n, t, low:high], h_send.at[n, i], h_recv.at[n, i],
             partner if n == 0 else z_from, s,
         )
 
-    for t in range(last):
+    hops_x = [hop(0, t) for t in range(1, nb)] + [hop(0, 0, 0, HB), hop(0, 0, HB, BLK)]
+    hops_z = [hop(1, v) for v in range(nb)]
+
+    for t in range(1, nb):
         par[block(t), :] = gram(stack(cor_x, t, nb, t * BLK, (t + 1) * BLK), eff[0, t * BLK :])
     both(stage4, last)
-    par[last * BLK : split, :] = gram(got(cor_x, last, last * BLK, split), eff[0, block(last)])
-
-    @pl.when(has_from)
-    def _():
-        for c in e_z:
-            c.wait_recv()
-        for t in range(last):
+    par[:HB, :] = gram(stack(cor_x, 0, nb, 0, HB), eff[0])
+
+    @pl.when(has_from)
+    def _():
+        e_z[0].wait_recv()
+        par[:HB, :] += gram(got(cor_z, 0, 0, HB), eff[2, block(0)])
+
+    for t in range(1, last):
+        @pl.when(has_from)
+        def _():
+            e_z[t].wait_recv()
             par[block(t), :] += gram(stack(cor_z, 0, t + 1, t * BLK, (t + 1) * BLK), eff[2, : (t + 1) * BLK])
 
-    for t in range(last):
         hop_out[0, t] = par[block(t), :].astype(BF16)
-        hop(0, t).start()
-
-    @pl.when(has_from)
-    def _():
-        stage3(late_z[0])
-        stage3(late_z[1])
-        par[last * BLK : split, :] += gram(stack(cor_z, 0, last, last * BLK, split), eff[2, : last * BLK])
-
-    for c in e_x:
-        c.wait_recv()
-
-    @pl.when(has_from)
-    def _():
-        for v in range(last):
-            far[block(v), :] = dot(got(cor_z, v, v * BLK, split), eff[1, v * BLK : split])
-        for v in range(2, nb):
-            stage3(late_z[v])
-
-    stage3(late_x)
-
-    @pl.when(has_from)
-    def _():
-        for v in range(nb):
-            stage4(late_z[v])
-            if v < last:
-                hop_out[1, v] = (far[block(v), :] + dot(got(cor_z, v, split, nb * BLK), eff[1, split:])).astype(BF16)
-            else:
-                hop_out[1, v] = dot(got(cor_z, v, last * BLK, nb * BLK), eff[1, last * BLK :]).astype(BF16)
-            hop(1, v).start()
-
-    stage4(late_x)
-    par[split:, :] = gram(got(cor_x, last, split, nb * BLK), eff[0, block(last)])
-
-    @pl.when(has_from)
-    def _():
-        par[split:, :] += gram(stack(cor_z, 0, last, split, nb * BLK), eff[2, : last * BLK])
-        par[block(last), :] += gram(got(cor_z, last, last * BLK, nb * BLK), eff[2, block(last)])
+        hops_x[t - 1].start()
+
+    hop_out[0, 0, :HB] = par[:HB, :].astype(BF16)
+    hops_x[nb - 1].start()
+    e_x[last].wait_recv()
+    for v in range(last - 1, 0, -1):
+        e_x[v].wait_recv()
+
+        @pl.when(has_from)
+        def _():
+            hop_out[1, v] = dot(got(cor_z, v, v * BLK, nb * BLK), eff[1, v * BLK :]).astype(BF16)
+            hops_z[v].start()
+
+    @pl.when(has_from)
+    def _():
+        e_z[last].wait_recv()
+        par[block(last), :] += gram(stack(cor_z, 0, last, last * BLK, nb * BLK), eff[2, : last * BLK])
+        far[block(0), :] = dot(got(cor_z, 0, BLK, nb * BLK), eff[1, BLK:])
+        stage3(late_z)
+        stage3(late_w)
+
+    e_x[0].wait_recv()
+
+    @pl.when(has_from)
+    def _():
+        stage4(late_z)
+        hop_out[1, 0] = (far[block(0), :] + dot(got(cor_z, 0, 0, BLK), eff[1, block(0)])).astype(BF16)
+        hops_z[0].start()
+        stage4(late_w)
+        corr = got(cor_w, 0, 0, BLK)
+        hop_out[1, last] = gram(corr, eff[1, block(last)]).astype(BF16)
+        hops_z[last].start()
+        par[block(last), :] += dot(corr, eff[2, block(last)])
 
     hop_out[0, last] = par[block(last), :].astype(BF16)
-    hop(0, last).start()
+    hops_x[last - 1].start()
+    for group in X[nb]:
+        stage3(group)
+    for group in X[nb]:
+        stage4(group)
+    par[HB:BLK, :] = gram(stack(cor_x, 0, nb, HB, BLK), eff[0])
+
+    @pl.when(has_from)
+    def _():
+        par[HB:BLK, :] += gram(got(cor_z, 0, HB, BLK), eff[2, block(0)])
+
+    hop_out[0, 0, HB:] = par[HB:BLK, :].astype(BF16)
+    hops_x[nb].start()
     for u in range(nb):
-        acc[block(u), :] += dot(got(cor_x, u, 0, (u + 1) * BLK), eff[1, : (u + 1) * BLK])
-    for u in range(nb - 1, -1, -1):
-        hop(0, nb - 1 - u).wait_recv()
-        out_ref[at_block(mine(u)), :] = acc[block(u), :] + hop_in[0, nb - 1 - u].astype(F32)
+        out_ref[at_block(mine(u)), :] = acc[block(u), :] + dot(got(cor_x, u, 0, (u + 1) * BLK), eff[1, : (u + 1) * BLK])
+    for t in range(1, nb):
+        hops_x[t - 1].wait_recv()
+        out_ref[at_block(other(t)), :] += hop_in[0, t].astype(F32)
 
     @pl.when(has_to)
     def _():
-        for v in range(nb):
-            hop(1, v).wait_recv()
+        for v in list(range(last - 1, -1, -1)) + [last]:
+            hops_z[v].wait_recv()
             out_ref[at_block(mine(v)), :] += hop_in[1, v].astype(F32)
+
+    hops_x[nb - 1].wait_recv()
+    hops_x[nb].wait_recv()
+    out_ref[at_block(other(0)), :] += hop_in[0, 0].astype(F32)
 
     for c in to_partner:
         c.wait_send()
@@ -433,19 +474,19 @@
         for c in to_next:
             c.wait_send()
 
-    for group in X + [L]:
+    for group in sum(X, [L]):
         for c in (to_core(group), to_cross(group), share(group)):
             c.wait_send()
-    for t in range(nb):
-        hop(0, t).wait_send()
-
-    @pl.when(has_from)
-    def _():
-        for group in Z:
+    for c in hops_x:
+        c.wait_send()
+
+    @pl.when(has_from)
+    def _():
+        for group in sum(Z + W, []):
             for c in (to_core(group), to_cross(group), share(group)):
                 c.wait_send()
-        for t in range(nb):
-            hop(1, t).wait_send()
+        for c in hops_z:
+            c.wait_send()
 
 
 def body(n_genome, n_samp, dosage, effects, depth):
@@ -455,12 +496,13 @@
     half = samples // 2
     dma = pltpu.SemaphoreType.DMA
     pairs = nb * (nb + 1) // 2
-    groups_x, groups_z = make_groups(nb)
-    n_groups = len(groups_x) + len(groups_z) + 1
-
-    def pair_of(kind, lead, dtype, lead_l=()):
+    n_groups = 1 + sum(len(step) for steps in make_groups(nb) for step in steps)
+
+    def pair_of(kind, lead, dtype):
         wide = pltpu.VMEM((nb,) + lead + (HB, variants), dtype)
-        return [wide, wide, pltpu.VMEM((pairs,) + lead + (HB, BLK), kind)]
+        return [
+            wide, wide, pltpu.VMEM((1,) + lead + (HB, BLK), dtype), pltpu.VMEM((pairs,) + lead + (HB, BLK), kind),
+        ]
 
     return pl.pallas_call(
         functools.partial(kernel, n_genome, n_samp, nb, half, 1.0 / (samples * n_samp)),
@@ -493,7 +535,7 @@
             dma((nb + len(PARTS),)), dma((nb + len(PARTS),)),
             dma((nb,)), dma((nb,)), dma((nb,)), dma((nb,)), dma((2,)), dma((2,)),
             dma((n_groups,)), dma((n_groups,)), dma((n_groups,)), dma((n_groups,)), dma((n_groups,)), dma((n_groups,)),
-            dma((2, nb)), dma((2, nb)),
+            dma((2, nb + 1)), dma((2, nb + 1)),
         ],
         compiler_params=pltpu.CompilerParams(
             collective_id=0, has_side_effects=True, vmem_limit_bytes=60 * 1024 * 1024

time: 113 us -> 110 us (0.973)
  Pallas kernels: 112 us -> 109 us
    pallas_call x1, Pallas kernels: 112 us -> 109 us  [body(): pl.pallas_call(functools.partial(kernel, n_genome, n_samp, nb, half, 1.0...]
where the time goes in v4:
time: 110 us
  Pallas kernels  109 us (99%)
    pallas_call x1, Pallas kernels, body(): pl.pallas_call(functools.partial(kernel, n_genome, n_samp, nb, half, 1.0...  109 us

profile of v4, /device:TPU:0, one launch (start us, length us, event | category | flops | bytes accessed | tf_op | source)
XLA Modules:
  0.0 110.3 jit_solution(15426185309125884819)
XLA Ops:
  0.0 109.5 %shard_map.37 = f32[1024,128]{1,0:T(8,128)S(1)} custom-call(bf16[4096,1024]{1,0:T(8,128)(2,1)} %x_ref.1, bf16[1024,128]{1,0:T(8,128)(2,1)} %e_ref.1, s32[4]{0:T(128)} %depth_ref.1), custom_call_target="tpu_custom_call" | custom-call | flops 10737418240 | bytes 16777216 | tf_op jit(solution)/shard_map/pallas_call | solution.py:507
  109.5 0.8 copy.5

commit v5 on v4

--- a/solution.py
+++ b/solution.py
@@ -29,22 +29,22 @@
         return t * BLK, (t + 1) * BLK
 
     x = [[(t, nb) + cols(t)] for t in range(1, nb)] + [[(0, nb, 0, HB)]]
-    x += [[(u, u + 2, HB, BLK) for u in range(0, nb, 2)]]
     z = [[(0, t) + cols(t)] + ([(t - 1, t) + cols(t - 1)] if t > 1 else []) for t in range(1, nb)]
-    z += [[(0, 1, 0, HB)], [(0, 1, HB, BLK)]]
-    w = [[(0, 1, 0, HB)], [(0, 1, HB, BLK)]]
-    return x, z, w
+    z += [[(0, 1, 0, HB)]]
+    spots = [0, nb * BLK // 2, nb * BLK, (nb + 1) * BLK, (nb + 2) * BLK, (nb + 3) * BLK]
+    late = [[(0, 1) + spot] for spot in zip(spots[:-1], spots[1:])]
+    return x, z, late
 
 
 def kernel(
     n_genome, n_samp, nb, half, scale,
     x_ref, e_ref, depth_ref, out_ref,
     d_ref, dep, own, xbuf, zbuf, eff,
-    sum_x, sum_z, sum_w, sum_l, cin_x, cin_z, cin_w, cin_l, yo_x, yo_z, yo_w, yo_l, yi_x, yi_z, yi_w, yi_l,
-    cor_x, cor_z, cor_w, cor_l,
-    acc, par, far, hop_out, hop_in,
+    sum_x, sum_z, sum_t, sum_l, cin_x, cin_z, cin_t, cin_l, yo_x, yo_z, yo_t, yo_l, yi_x, yi_z, yi_t, yi_l,
+    cor_x, cor_z, cor_t, cor_l,
+    acc, par, far, hop_out, hop_in, pair_e, mate_far, last_sum, last_out, last_in,
     own_sem, own_e_sem, x_send, x_recv, z_send, z_recv, ex_send, ex_recv, ez_send, ez_recv, ds_send, ds_recv,
-    a_send, a_recv, b_send, b_recv, c_send, c_recv, h_send, h_recv,
+    a_send, a_recv, b_send, b_recv, c_send, c_recv, h_send, h_recv, m_send, m_recv, l_send, l_recv,
 ):
     g = lax.axis_index("genome")
     s = lax.axis_index("samp")
@@ -82,7 +82,8 @@
     barrier = pltpu.get_barrier_semaphore()
     for mate in (core_mate, cross_mate):
         pl.semaphore_signal(barrier, inc=1, device_id=(g, mate), device_id_type=MESH)
-    pl.semaphore_signal(barrier, inc=1, device_id=(partner, s), device_id_type=MESH)
+    for mate in (s, core_mate):
+        pl.semaphore_signal(barrier, inc=1, device_id=(partner, mate), device_id_type=MESH)
 
     @pl.when(has_from)
     def _():
@@ -104,7 +105,7 @@
     for u in range(nb):
         d_ref[u : u + 1, :] = jnp.full((1, BLK), depth_ref[mine(u)].astype(F32))
     pl.semaphore_wait(
-        barrier, 3 + has_from.astype(jnp.int32) + has_to.astype(jnp.int32)
+        barrier, 4 + has_from.astype(jnp.int32) + has_to.astype(jnp.int32)
     )
 
     pieces = []
@@ -140,9 +141,14 @@
     ]
     d_x = remote(d_ref, dep.at[0], ds_send.at[0], ds_recv.at[0], partner, s)
     d_z = remote(d_ref, dep.at[1], ds_send.at[1], ds_recv.at[1], z_to, s)
+    e_mate = [
+        remote(e_ref.at[at_block(mine(u)), :], pair_e.at[u * BLK : (u + 1) * BLK], m_send.at[u], m_recv.at[u], g, core_mate)
+        for u in range(nb)
+    ]
+    f_mate = remote(eff.at[2, :BLK], mate_far, m_send.at[nb], m_recv.at[nb], g, core_mate)
     to_partner = [d_x] + x_copies + x_last + e_x[::-1]
     to_next = [d_z] + z_copies + z_last + e_z
-    for c in to_partner:
+    for c in to_partner + e_mate:
         c.start()
 
     @pl.when(has_to)
@@ -159,10 +165,12 @@
             counter[0] += len(step)
         return out
 
-    groups_x, groups_z, groups_w = make_groups(nb)
+    groups_x, groups_z, groups_t = make_groups(nb)
     X = label(groups_x, (sum_x, cin_x, yo_x, yi_x, cor_x))
     Z = label(groups_z, (sum_z, cin_z, yo_z, yi_z, cor_z))
-    W = label(groups_w, (sum_w, cin_w, yo_w, yi_w, cor_w))
+    T = label(groups_t, (sum_t, cin_t, yo_t, yi_t, cor_t))
+    late_x, (late_z, late_w, early_w) = [T[0][0], T[1][0]], [step[0] for step in T[2:]]
+    SPOT_Z, SPOT_W, SPOT_V = nb * BLK, (nb + 1) * BLK, (nb + 2) * BLK
     L = label([[(0, nb * (nb + 1) // 2, 0, BLK)]], (sum_l, cin_l, yo_l, yi_l, cor_l))[0][0]
 
     def to_core(group):
@@ -290,7 +298,7 @@
         lax.fori_loop(0, nb, local_row, 0)
 
     def from_groups(k):
-        return Z[k] + (W[k - last] if k >= last else [])
+        return Z[k] + ([early_w] if k == last else [])
 
     def both(stage, k):
         for group in X[k]:
@@ -316,8 +324,9 @@
                     z_grams(k, k + 1, k, left, right)
             else:
                 z_grams(0, 1, 0, left, right)
-                full = gram(xbuf[last], zbuf[last, :, left:right])
-                put(sum_w, 0, left, right, full * z_weight(last, last, HB))
+                full = gram(zbuf[last, :, left:right], xbuf[last]) * z_weight(last, last, BLK)
+                for h in range(2):
+                    sum_t[0, h, :, SPOT_V : SPOT_V + BLK] = full[h * HB // 2 : (h + 1) * HB // 2]
             for group in from_groups(k):
                 stage1(group)
 
@@ -332,45 +341,44 @@
             both(stage3, 1)
             both(stage4, 1)
 
-    late_z, late_w = Z[nb][0], W[1][0]
     for n, (low, high) in enumerate(pieces):
         final = n == len(pieces) - 1
 
-        def add(ref, a, value, factor):
+        def add(left, value, factor):
             for h in range(2):
-                part = value[h * HB : (h + 1) * HB]
+                part = value[h * HB // 2 : (h + 1) * HB // 2]
                 if n:
-                    part = ref[a, h, :, HB:BLK] + part
-                ref[a, h, :, HB:BLK] = part * factor if final else part
+                    part = sum_t[0, h, :, left : left + BLK] + part
+                sum_t[0, h, :, left : left + BLK] = part * factor if final else part
 
         if n == 1:
             both(stage3, 2)
         x_last[n].wait_recv()
+        piece = xbuf[0, low:high, HB:].T
 
         @pl.when(has_from)
         def _():
-            full = gram(zbuf[0, low:high], xbuf[0, low:high, HB:])
-            add(sum_z, 0, full, z_weight(0, 0, HB) if final else None)
+            add(SPOT_Z, dot(piece, zbuf[0, low:high]), z_weight(0, 0, BLK) if final else None)
             if final:
                 stage1(late_z)
             z_last[n].wait_recv()
-            full = gram(xbuf[last, low:high], zbuf[last, low:high, HB:])
-            add(sum_w, 0, full, z_weight(last, last, HB) if final else None)
+            full = dot(zbuf[last, low:high, HB:].T, xbuf[last, low:high])
+            add(SPOT_W, full, z_weight(last, last, BLK) if final else None)
             if final:
                 stage1(late_w)
 
         for u in range(nb):
-            full = gram(own[u, half_rows(q, low, high), :], xbuf[0, low:high, HB:])
-            add(sum_x, u, full, x_weight(0, u, HB) if final else None)
-            if final and u % 2:
-                stage1(X[nb][u // 2])
+            full = dot(piece, own[u, half_rows(q, low, high), :])
+            add(u * BLK, full, x_weight(0, u, BLK) if final else None)
+            if final and u % (nb // 2) == nb // 2 - 1:
+                stage1(late_x[u // (nb // 2)])
 
     @pl.when(has_from)
     def _():
         stage2(late_z)
         stage2(late_w)
 
-    for group in X[nb]:
+    for group in late_x:
         stage2(group)
     both(stage4, 2)
     both(stage3, last)
@@ -382,8 +390,18 @@
             partner if n == 0 else z_from, s,
         )
 
-    hops_x = [hop(0, t) for t in range(1, nb)] + [hop(0, 0, 0, HB), hop(0, 0, HB, BLK)]
-    hops_z = [hop(1, v) for v in range(nb)]
+    hops_x = [hop(0, t) for t in range(1, nb)] + [hop(0, 0, 0, HB)]
+    hops_last = [
+        remote(last_out.at[n], last_in.at[core], l_send.at[n], l_recv.at[core], partner, to)
+        for n, to in enumerate((s, core_mate))
+    ]
+    last_arrivals = [
+        remote(last_out.at[0], last_in.at[n], l_send.at[0], l_recv.at[n], partner, s) for n in range(2)
+    ]
+    hops_z = [hop(1, v) for v in range(last)] + [hop(1, last, 0, HB), hop(1, last, HB, BLK)]
+
+    def late(left, right):
+        return cor_t[0, :, :, left:right].reshape(HB, right - left)
 
     for t in range(1, nb):
         par[block(t), :] = gram(stack(cor_x, t, nb, t * BLK, (t + 1) * BLK), eff[0, t * BLK :])
@@ -393,6 +411,7 @@
     @pl.when(has_from)
     def _():
         e_z[0].wait_recv()
+        f_mate.start()
         par[:HB, :] += gram(got(cor_z, 0, 0, HB), eff[2, block(0)])
 
     for t in range(1, last):
@@ -407,6 +426,12 @@
     hop_out[0, 0, :HB] = par[:HB, :].astype(BF16)
     hops_x[nb - 1].start()
     e_x[last].wait_recv()
+
+    @pl.when(has_from)
+    def _():
+        hop_out[1, last, :HB] = dot(late(SPOT_V, SPOT_V + BLK), eff[1, block(last)]).astype(BF16)
+        hops_z[last].start()
+
     for v in range(last - 1, 0, -1):
         e_x[v].wait_recv()
 
@@ -417,9 +442,11 @@
 
     @pl.when(has_from)
     def _():
-        e_z[last].wait_recv()
         par[block(last), :] += gram(stack(cor_z, 0, last, last * BLK, nb * BLK), eff[2, : last * BLK])
         far[block(0), :] = dot(got(cor_z, 0, BLK, nb * BLK), eff[1, BLK:])
+
+    @pl.when(has_from)
+    def _():
         stage3(late_z)
         stage3(late_w)
 
@@ -427,31 +454,74 @@
 
     @pl.when(has_from)
     def _():
+        e_z[last].wait_recv()
+        far[block(0), :] += dot(got(cor_z, 0, 0, HB), eff[1, :HB])
+        par[block(last), :] += gram(late(SPOT_V, SPOT_V + BLK), eff[2, last * BLK : last * BLK + HB])
         stage4(late_z)
-        hop_out[1, 0] = (far[block(0), :] + dot(got(cor_z, 0, 0, BLK), eff[1, block(0)])).astype(BF16)
+        hop_out[1, 0] = (far[block(0), :] + gram(late(SPOT_Z, SPOT_Z + BLK), eff[1, HB:BLK])).astype(BF16)
         hops_z[0].start()
         stage4(late_w)
-        corr = got(cor_w, 0, 0, BLK)
-        hop_out[1, last] = gram(corr, eff[1, block(last)]).astype(BF16)
-        hops_z[last].start()
-        par[block(last), :] += dot(corr, eff[2, block(last)])
+        corr = late(SPOT_W, SPOT_W + BLK)
+        par[block(last), :] += gram(corr, eff[2, last * BLK + HB :])
+        hop_out[1, last, HB:] = dot(corr, eff[1, block(last)]).astype(BF16)
+        hops_z[nb].start()
 
     hop_out[0, last] = par[block(last), :].astype(BF16)
     hops_x[last - 1].start()
-    for group in X[nb]:
-        stage3(group)
-    for group in X[nb]:
+    for c in e_mate:
+        c.wait_recv()
+
+    def last_rows(left, right):
+        return cor_t[0, core, :, left:right]
+
+    @pl.when(has_from)
+    def _():
+        f_mate.wait_recv()
+        rows = last_rows(SPOT_Z, SPOT_Z + BLK)
+        last_sum[0] = dot(rows, eff[2, :BLK])
+        last_sum[1] = dot(rows, mate_far[...])
+
+    @pl.when(jnp.logical_not(has_from))
+    def _():
+        last_sum[...] = jnp.zeros_like(last_sum)
+
+    middle = nb * BLK // 2
+    stage3(late_x[0])
+    last_sum[0] += dot(last_rows(0, middle), eff[0, :middle])
+    last_sum[1] += dot(last_rows(0, middle), pair_e[:middle])
+    stage3(late_x[1])
+    for n, effects in enumerate((eff.at[0], pair_e)):
+        value = last_sum[n] + dot(last_rows(middle, nb * BLK), effects[middle:])
+        last_out[n] = value.astype(BF16)
+        hops_last[n].start()
+
+    for group in late_x:
         stage4(group)
-    par[HB:BLK, :] = gram(stack(cor_x, 0, nb, HB, BLK), eff[0])
-
-    @pl.when(has_from)
-    def _():
-        par[HB:BLK, :] += gram(got(cor_z, 0, HB, BLK), eff[2, block(0)])
-
-    hop_out[0, 0, HB:] = par[HB:BLK, :].astype(BF16)
-    hops_x[nb].start()
+    acc[...] += gram(late(0, nb * BLK), eff[1, HB:BLK])
     for u in range(nb):
-        out_ref[at_block(mine(u)), :] = acc[block(u), :] + dot(got(cor_x, u, 0, (u + 1) * BLK), eff[1, : (u + 1) * BLK])
+        early = acc[block(u), :] + dot(got(cor_x, u, 0, HB), eff[1, :HB])
+        if u:
+            early += dot(got(cor_x, u, BLK, (u + 1) * BLK), eff[1, BLK : (u + 1) * BLK])
+        out_ref[at_block(mine(u)), :] = early
+    for c in to_partner + e_mate:
+        c.wait_send()
+
+    @pl.when(has_to)
+    def _():
+        for c in to_next:
+            c.wait_send()
+
+    for group in sum(X, [L]) + late_x:
+        for c in (to_core(group), to_cross(group), share(group)):
+            c.wait_send()
+
+    @pl.when(has_from)
+    def _():
+        f_mate.wait_send()
+        for group in sum(Z, [late_z, late_w, early_w]):
+            for c in (to_core(group), to_cross(group), share(group)):
+                c.wait_send()
+
     for t in range(1, nb):
         hops_x[t - 1].wait_recv()
         out_ref[at_block(other(t)), :] += hop_in[0, t].astype(F32)
@@ -460,31 +530,22 @@
     def _():
         for v in list(range(last - 1, -1, -1)) + [last]:
             hops_z[v].wait_recv()
+            if v == last:
+                hops_z[nb].wait_recv()
             out_ref[at_block(mine(v)), :] += hop_in[1, v].astype(F32)
 
     hops_x[nb - 1].wait_recv()
-    hops_x[nb].wait_recv()
-    out_ref[at_block(other(0)), :] += hop_in[0, 0].astype(F32)
-
-    for c in to_partner:
+    first = pl.ds(pl.multiple_of(other(0) * BLK, BLK), HB)
+    out_ref[first, :] += hop_in[0, 0, :HB].astype(F32)
+    for n, c in enumerate(last_arrivals):
+        c.wait_recv()
+        rows = pl.ds(pl.multiple_of(other(0) * BLK + HB + n * (HB // 2), HB // 2), HB // 2)
+        out_ref[rows, :] += last_in[n].astype(F32)
+    for c in hops_x + hops_last:
         c.wait_send()
 
-    @pl.when(has_to)
-    def _():
-        for c in to_next:
-            c.wait_send()
-
-    for group in sum(X, [L]):
-        for c in (to_core(group), to_cross(group), share(group)):
-            c.wait_send()
-    for c in hops_x:
-        c.wait_send()
-
-    @pl.when(has_from)
-    def _():
-        for group in sum(Z + W, []):
-            for c in (to_core(group), to_cross(group), share(group)):
-                c.wait_send()
+    @pl.when(has_from)
+    def _():
         for c in hops_z:
             c.wait_send()
 
@@ -501,7 +562,7 @@
     def pair_of(kind, lead, dtype):
         wide = pltpu.VMEM((nb,) + lead + (HB, variants), dtype)
         return [
-            wide, wide, pltpu.VMEM((1,) + lead + (HB, BLK), dtype), pltpu.VMEM((pairs,) + lead + (HB, BLK), kind),
+            wide, wide, pltpu.VMEM((1,) + lead + (HB // 2, (nb + 3) * BLK), dtype), pltpu.VMEM((pairs,) + lead + (HB, BLK), kind),
         ]
 
     return pl.pallas_call(
@@ -530,12 +591,17 @@
             pltpu.VMEM((variants, traits), F32),
             pltpu.VMEM((2, nb, BLK, traits), BF16),
             pltpu.VMEM((2, nb, BLK, traits), BF16),
+            pltpu.VMEM((variants, traits), BF16),
+            pltpu.VMEM((BLK, traits), BF16),
+            pltpu.VMEM((2, HB // 2, traits), F32),
+            pltpu.VMEM((2, HB // 2, traits), BF16),
+            pltpu.VMEM((2, HB // 2, traits), BF16),
             dma((nb,)), dma((nb,)),
             dma((nb + len(PARTS),)), dma((nb + len(PARTS),)),
             dma((nb + len(PARTS),)), dma((nb + len(PARTS),)),
             dma((nb,)), dma((nb,)), dma((nb,)), dma((nb,)), dma((2,)), dma((2,)),
             dma((n_groups,)), dma((n_groups,)), dma((n_groups,)), dma((n_groups,)), dma((n_groups,)), dma((n_groups,)),
-            dma((2, nb + 1)), dma((2, nb + 1)),
+            dma((2, nb + 1)), dma((2, nb + 1)), dma((nb + 1,)), dma((nb + 1,)), dma((2,)), dma((2,)),
         ],
         compiler_params=pltpu.CompilerParams(
             collective_id=0, has_side_effects=True, vmem_limit_bytes=60 * 1024 * 1024

time: 110 us -> 110 us (level)
  no operation moved by 1% of the time
where the time goes in v5:
time: 110 us; the launch traced here: 109 us
  Pallas kernels  109 us (99%)
    pallas_call x1, Pallas kernels, body(): pl.pallas_call(functools.partial(kernel, n_genome, n_samp, nb, half, 1.0...  109 us

profile of v5, /device:TPU:0, one launch (start us, length us, event | category | flops | bytes accessed | tf_op | source)
XLA Modules:
  0.0 109.4 jit_solution(14378823764792112618)
XLA Ops:
  0.0 108.6 %shard_map.37 = f32[1024,128]{1,0:T(8,128)S(1)} custom-call(bf16[4096,1024]{1,0:T(8,128)(2,1)} %x_ref.1, bf16[1024,128]{1,0:T(8,128)(2,1)} %e_ref.1, s32[4]{0:T(128)} %depth_ref.1), custom_call_target="tpu_custom_call" | custom-call | flops 10737418240 | bytes 16777216 | tf_op jit(solution)/shard_map/pallas_call | solution.py:568
  108.6 0.8 copy.5

commit v6 on v5

--- a/solution.py
+++ b/solution.py
@@ -309,6 +309,14 @@
             for group in from_groups(k):
                 stage(group)
 
+    def par_rows(t):
+        par[block(t), :] = gram(stack(cor_x, t, nb, t * BLK, (t + 1) * BLK), eff[0, t * BLK :])
+
+    def finish(groups):
+        for group in groups:
+            for c in (to_core(group), to_cross(group), share(group)):
+                c.wait_send()
+
     for k in range(nb):
         t, left, right = (k + 1, 0, BLK) if k < last else (0, 0, HB)
         x_copies[k].wait_recv()
@@ -337,9 +345,11 @@
             stage4(L)
             local_products()
             both(stage4, 0)
+            par_rows(1)
         if k == 2:
             both(stage3, 1)
             both(stage4, 1)
+            par_rows(2)
 
     for n, (low, high) in enumerate(pieces):
         final = n == len(pieces) - 1
@@ -351,8 +361,30 @@
                     part = sum_t[0, h, :, left : left + BLK] + part
                 sum_t[0, h, :, left : left + BLK] = part * factor if final else part
 
+        if n == 0:
+            for c in e_mate:
+                c.wait_recv()
+            for c in e_mate + to_partner[:last]:
+                c.wait_send()
+            finish(sum(X[: last - 1], [L]))
+
+            @pl.when(has_to)
+            def _():
+                for c in to_next[:last]:
+                    c.wait_send()
+
+            @pl.when(has_from)
+            def _():
+                finish(sum(Z[: last - 1], []))
+
         if n == 1:
             both(stage3, 2)
+        if n == 2:
+            both(stage4, 2)
+            par_rows(last)
+            both(stage3, last)
+        if n == 3:
+            both(stage4, last)
         x_last[n].wait_recv()
         piece = xbuf[0, low:high, HB:].T
 
@@ -380,8 +412,6 @@
 
     for group in late_x:
         stage2(group)
-    both(stage4, 2)
-    both(stage3, last)
 
     def hop(n, t, low=0, high=BLK):
         i = nb if low else t
@@ -403,9 +433,6 @@
     def late(left, right):
         return cor_t[0, :, :, left:right].reshape(HB, right - left)
 
-    for t in range(1, nb):
-        par[block(t), :] = gram(stack(cor_x, t, nb, t * BLK, (t + 1) * BLK), eff[0, t * BLK :])
-    both(stage4, last)
     par[:HB, :] = gram(stack(cor_x, 0, nb, 0, HB), eff[0])
 
     @pl.when(has_from)
@@ -442,13 +469,26 @@
 
     @pl.when(has_from)
     def _():
+        stage3(late_z)
         par[block(last), :] += gram(stack(cor_z, 0, last, last * BLK, nb * BLK), eff[2, : last * BLK])
+        stage3(late_w)
         far[block(0), :] = dot(got(cor_z, 0, BLK, nb * BLK), eff[1, BLK:])
 
-    @pl.when(has_from)
-    def _():
-        stage3(late_z)
-        stage3(late_w)
+    for u in range(1, nb):
+        acc[block(u), :] += dot(got(cor_x, u, BLK, (u + 1) * BLK), eff[1, BLK : (u + 1) * BLK])
+    for c in to_partner[last:-1]:
+        c.wait_send()
+    finish(sum(X[last - 1 :], []))
+
+    @pl.when(has_to)
+    def _():
+        for c in to_next[last:-1]:
+            c.wait_send()
+
+    @pl.when(has_from)
+    def _():
+        f_mate.wait_send()
+        finish(sum(Z[last - 1 :], [early_w]))
 
     e_x[0].wait_recv()
 
@@ -468,9 +508,6 @@
 
     hop_out[0, last] = par[block(last), :].astype(BF16)
     hops_x[last - 1].start()
-    for c in e_mate:
-        c.wait_recv()
-
     def last_rows(left, right):
         return cor_t[0, core, :, left:right]
 
@@ -485,6 +522,7 @@
     def _():
         last_sum[...] = jnp.zeros_like(last_sum)
 
+    acc[...] += dot(stack(cor_x, 0, nb, 0, HB), eff[1, :HB])
     middle = nb * BLK // 2
     stage3(late_x[0])
     last_sum[0] += dot(last_rows(0, middle), eff[0, :middle])
@@ -497,30 +535,20 @@
 
     for group in late_x:
         stage4(group)
-    acc[...] += gram(late(0, nb * BLK), eff[1, HB:BLK])
+    value = gram(late(0, nb * BLK), eff[1, HB:BLK])
     for u in range(nb):
-        early = acc[block(u), :] + dot(got(cor_x, u, 0, HB), eff[1, :HB])
-        if u:
-            early += dot(got(cor_x, u, BLK, (u + 1) * BLK), eff[1, BLK : (u + 1) * BLK])
-        out_ref[at_block(mine(u)), :] = early
-    for c in to_partner + e_mate:
-        c.wait_send()
+        out_ref[at_block(mine(u)), :] = acc[block(u), :] + value[block(u)]
+    to_partner[-1].wait_send()
 
     @pl.when(has_to)
     def _():
-        for c in to_next:
-            c.wait_send()
-
-    for group in sum(X, [L]) + late_x:
-        for c in (to_core(group), to_cross(group), share(group)):
-            c.wait_send()
-
-    @pl.when(has_from)
-    def _():
-        f_mate.wait_send()
-        for group in sum(Z, [late_z, late_w, early_w]):
-            for c in (to_core(group), to_cross(group), share(group)):
-                c.wait_send()
+        to_next[-1].wait_send()
+
+    finish(late_x)
+
+    @pl.when(has_from)
+    def _():
+        finish([late_z, late_w])
 
     for t in range(1, nb):
         hops_x[t - 1].wait_recv()

time: 110 us -> 110 us (level)
  no operation moved by 1% of the time
where the time goes in v6:
time: 110 us; the launch traced here: 109 us
  Pallas kernels  109 us (99%)
    pallas_call x1, Pallas kernels, body(): pl.pallas_call(functools.partial(kernel, n_genome, n_samp, nb, half, 1.0...  109 us

profile of v6, /device:TPU:0, one launch (start us, length us, event | category | flops | bytes accessed | tf_op | source)
XLA Modules:
  0.0 109.4 jit_solution(1880644068421463673)
XLA Ops:
  0.0 108.6 %shard_map.37 = f32[1024,128]{1,0:T(8,128)S(1)} custom-call(bf16[4096,1024]{1,0:T(8,128)(2,1)} %x_ref.1, bf16[1024,128]{1,0:T(8,128)(2,1)} %e_ref.1, s32[4]{0:T(128)} %depth_ref.1), custom_call_target="tpu_custom_call" | custom-call | flops 10737418240 | bytes 16777216 | tf_op jit(solution)/shard_map/pallas_call | solution.py:596
  108.6 0.8 copy.5

commit v7 on v6

--- a/solution.py
+++ b/solution.py
@@ -33,7 +33,7 @@
     z += [[(0, 1, 0, HB)]]
     spots = [0, nb * BLK // 2, nb * BLK, (nb + 1) * BLK, (nb + 2) * BLK, (nb + 3) * BLK]
     late = [[(0, 1) + spot] for spot in zip(spots[:-1], spots[1:])]
-    return x, z, late
+    return x, z, late[-1:] + late[:-1]
 
 
 def kernel(
@@ -94,10 +94,10 @@
         pl.semaphore_signal(barrier, inc=1, device_id=(z_to, s), device_id_type=MESH)
 
     own_copies = [
-        pltpu.make_async_copy(x_ref.at[:, at_block(mine(u))], own.at[u], own_sem.at[u]) for u in range(nb)
+        pltpu.make_async_copy(x_ref.at[:, at_block(mine(u))], own.at[u], own_sem.at[0]) for u in range(nb)
     ]
     own_effects = [
-        pltpu.make_async_copy(e_ref.at[at_block(mine(u)), :], eff.at[0, u * BLK : (u + 1) * BLK], own_e_sem.at[u])
+        pltpu.make_async_copy(e_ref.at[at_block(mine(u)), :], eff.at[0, u * BLK : (u + 1) * BLK], own_e_sem.at[0])
         for u in range(nb)
     ]
     for c in own_copies + own_effects:
@@ -117,14 +117,14 @@
         src = pl.ds(pl.multiple_of(other(t) * BLK + left, HB), right - left)
         return remote(
             x_ref.at[half_rows(1 - q, low, high), src], xbuf.at[t, low:high, left:right],
-            x_send.at[n], x_recv.at[n], partner, s,
+            x_send.at[0], x_recv.at[n], partner, s,
         )
 
     def z_part(v, low, high, left, right, n):
         src = pl.ds(pl.multiple_of(mine(v) * BLK + left, HB), right - left)
         return remote(
             x_ref.at[half_rows(q, low, high), src], zbuf.at[v, low:high, left:right],
-            z_send.at[n], z_recv.at[n], z_to, s,
+            z_send.at[0], z_recv.at[n], z_to, s,
         )
 
     x_copies = [x_part(k + 1, 0, half, 0, BLK, k) for k in range(last)] + [x_part(0, 0, half, 0, HB, last)]
@@ -132,23 +132,20 @@
     x_last = [x_part(0, low, high, HB, BLK, nb + n) for n, (low, high) in enumerate(pieces)]
     z_last = [z_part(last, low, high, HB, BLK, nb + n) for n, (low, high) in enumerate(pieces)]
     e_x = [
-        remote(e_ref.at[at_block(other(t)), :], eff.at[1, t * BLK : (t + 1) * BLK], ex_send.at[t], ex_recv.at[t], partner, s)
+        remote(e_ref.at[at_block(other(t)), :], eff.at[1, t * BLK : (t + 1) * BLK], ex_send.at[0], ex_recv.at[t], partner, s)
         for t in range(nb)
     ]
     e_z = [
-        remote(e_ref.at[at_block(mine(v)), :], eff.at[2, v * BLK : (v + 1) * BLK], ez_send.at[v], ez_recv.at[v], z_to, s)
+        remote(e_ref.at[at_block(mine(v)), :], eff.at[2, v * BLK : (v + 1) * BLK], ez_send.at[0], ez_recv.at[v], z_to, s)
         for v in range(nb)
     ]
     d_x = remote(d_ref, dep.at[0], ds_send.at[0], ds_recv.at[0], partner, s)
     d_z = remote(d_ref, dep.at[1], ds_send.at[1], ds_recv.at[1], z_to, s)
-    e_mate = [
-        remote(e_ref.at[at_block(mine(u)), :], pair_e.at[u * BLK : (u + 1) * BLK], m_send.at[u], m_recv.at[u], g, core_mate)
-        for u in range(nb)
-    ]
-    f_mate = remote(eff.at[2, :BLK], mate_far, m_send.at[nb], m_recv.at[nb], g, core_mate)
+    e_mate = remote(eff.at[0], pair_e, m_send.at[0], m_recv.at[0], g, core_mate)
+    f_mate = remote(eff.at[2, :BLK], mate_far, m_send.at[1], m_recv.at[1], g, core_mate)
     to_partner = [d_x] + x_copies + x_last + e_x[::-1]
     to_next = [d_z] + z_copies + z_last + e_z
-    for c in to_partner + e_mate:
+    for c in to_partner:
         c.start()
 
     @pl.when(has_to)
@@ -168,8 +165,12 @@
     groups_x, groups_z, groups_t = make_groups(nb)
     X = label(groups_x, (sum_x, cin_x, yo_x, yi_x, cor_x))
     Z = label(groups_z, (sum_z, cin_z, yo_z, yi_z, cor_z))
-    T = label(groups_t, (sum_t, cin_t, yo_t, yi_t, cor_t))
-    late_x, (late_z, late_w, early_w) = [T[0][0], T[1][0]], [step[0] for step in T[2:]]
+    T = label(groups_t[:1], (sum_t, cin_t, yo_t, yi_t, cor_t))
+    early_w = T[0][0]
+    refs_t = early_w[1]
+    spots = groups_t[1:]
+    late_x = [(X[n][0][0], refs_t) + spots[n][0] for n in range(2)]
+    late_z, late_w = [(Z[n][0][0], refs_t) + spots[2 + n][0] for n in range(2)]
     SPOT_Z, SPOT_W, SPOT_V = nb * BLK, (nb + 1) * BLK, (nb + 2) * BLK
     L = label([[(0, nb * (nb + 1) // 2, 0, BLK)]], (sum_l, cin_l, yo_l, yi_l, cor_l))[0][0]
 
@@ -242,8 +243,9 @@
     def block(n):
         return slice(n * BLK, (n + 1) * BLK)
 
-    for c in own_copies + own_effects:
-        c.wait()
+    pltpu.make_async_copy(eff.at[0], eff.at[0], own_e_sem.at[0]).wait()
+    e_mate.start()
+    pltpu.make_async_copy(own, own, own_sem.at[0]).wait()
 
     def local_row(i, carry):
         def local_pair(j, carry):
@@ -362,16 +364,8 @@
                 sum_t[0, h, :, left : left + BLK] = part * factor if final else part
 
         if n == 0:
-            for c in e_mate:
-                c.wait_recv()
-            for c in e_mate + to_partner[:last]:
-                c.wait_send()
+            e_mate.wait()
             finish(sum(X[: last - 1], [L]))
-
-            @pl.when(has_to)
-            def _():
-                for c in to_next[:last]:
-                    c.wait_send()
 
             @pl.when(has_from)
             def _():
@@ -476,14 +470,14 @@
 
     for u in range(1, nb):
         acc[block(u), :] += dot(got(cor_x, u, BLK, (u + 1) * BLK), eff[1, BLK : (u + 1) * BLK])
-    for c in to_partner[last:-1]:
-        c.wait_send()
+    d_x.wait_send()
+    remote(xbuf, xbuf, x_send.at[0], x_recv.at[0], partner, s).wait_send()
     finish(sum(X[last - 1 :], []))
 
     @pl.when(has_to)
     def _():
-        for c in to_next[last:-1]:
-            c.wait_send()
+        d_z.wait_send()
+        remote(zbuf, zbuf, z_send.at[0], z_recv.at[0], z_to, s).wait_send()
 
     @pl.when(has_from)
     def _():
@@ -538,11 +532,11 @@
     value = gram(late(0, nb * BLK), eff[1, HB:BLK])
     for u in range(nb):
         out_ref[at_block(mine(u)), :] = acc[block(u), :] + value[block(u)]
-    to_partner[-1].wait_send()
+    remote(eff.at[1], eff.at[1], ex_send.at[0], ex_recv.at[0], partner, s).wait_send()
 
     @pl.when(has_to)
     def _():
-        to_next[-1].wait_send()
+        remote(eff.at[2], eff.at[2], ez_send.at[0], ez_recv.at[0], z_to, s).wait_send()
 
     finish(late_x)
 
@@ -585,7 +579,7 @@
     half = samples // 2
     dma = pltpu.SemaphoreType.DMA
     pairs = nb * (nb + 1) // 2
-    n_groups = 1 + sum(len(step) for steps in make_groups(nb) for step in steps)
+    n_groups = 2 + sum(len(step) for steps in make_groups(nb)[:2] for step in steps)
 
     def pair_of(kind, lead, dtype):
         wide = pltpu.VMEM((nb,) + lead + (HB, variants), dtype)
@@ -624,12 +618,12 @@
             pltpu.VMEM((2, HB // 2, traits), F32),
             pltpu.VMEM((2, HB // 2, traits), BF16),
             pltpu.VMEM((2, HB // 2, traits), BF16),
-            dma((nb,)), dma((nb,)),
-            dma((nb + len(PARTS),)), dma((nb + len(PARTS),)),
-            dma((nb + len(PARTS),)), dma((nb + len(PARTS),)),
-            dma((nb,)), dma((nb,)), dma((nb,)), dma((nb,)), dma((2,)), dma((2,)),
+            dma((1,)), dma((1,)),
+            dma((1,)), dma((nb + len(PARTS),)),
+            dma((1,)), dma((nb + len(PARTS),)),
+            dma((1,)), dma((nb,)), dma((1,)), dma((nb,)), dma((2,)), dma((2,)),
             dma((n_groups,)), dma((n_groups,)), dma((n_groups,)), dma((n_groups,)), dma((n_groups,)), dma((n_groups,)),
-            dma((2, nb + 1)), dma((2, nb + 1)), dma((nb + 1,)), dma((nb + 1,)), dma((2,)), dma((2,)),
+            dma((2, nb + 1)), dma((2, nb + 1)), dma((2,)), dma((2,)), dma((2,)), dma((2,)),
         ],
         compiler_params=pltpu.CompilerParams(
             collective_id=0, has_side_effects=True, vmem_limit_bytes=60 * 1024 * 1024

time: 110 us -> 109 us (level)
  no operation moved by 1% of the time
where the time goes in v7:
time: 109 us
  Pallas kernels  108 us (99%)
    pallas_call x1, Pallas kernels, body(): pl.pallas_call(functools.partial(kernel, n_genome, n_samp, nb, half, 1.0...  108 us

profile of v7, /device:TPU:0, one launch (start us, length us, event | category | flops | bytes accessed | tf_op | source)
XLA Modules:
  0.0 108.9 jit_solution(15352107772828560671)
XLA Ops:
  0.0 108.1 %shard_map.37 = f32[1024,128]{1,0:T(8,128)S(1)} custom-call(bf16[4096,1024]{1,0:T(8,128)(2,1)} %x_ref.1, bf16[1024,128]{1,0:T(8,128)(2,1)} %e_ref.1, s32[4]{0:T(128)} %depth_ref.1), custom_call_target="tpu_custom_call" | custom-call | flops 10737418240 | bytes 16777216 | tf_op jit(solution)/shard_map/pallas_call | solution.py:590
  108.1 0.8 copy.5

commit v8 on v7

--- a/solution.py
+++ b/solution.py
@@ -80,11 +80,11 @@
         return pl.ds(pl.multiple_of(which * half + low, 16), high - low)
 
     barrier = pltpu.get_barrier_semaphore()
+    for mate in (s, core_mate):
+        pl.semaphore_signal(barrier, inc=1, device_id=(partner, mate), device_id_type=MESH)
+
     for mate in (core_mate, cross_mate):
         pl.semaphore_signal(barrier, inc=1, device_id=(g, mate), device_id_type=MESH)
-    for mate in (s, core_mate):
-        pl.semaphore_signal(barrier, inc=1, device_id=(partner, mate), device_id_type=MESH)
-
     @pl.when(has_from)
     def _():
         pl.semaphore_signal(barrier, inc=1, device_id=(z_from, s), device_id_type=MESH)
@@ -410,7 +410,7 @@
     def hop(n, t, low=0, high=BLK):
         i = nb if low else t
         return remote(
-            hop_out.at[n, t, low:high], hop_in.at[n, t, low:high], h_send.at[n, i], h_recv.at[n, i],
+            hop_out.at[n, t, low:high], hop_in.at[n, t, low:high], h_send.at[n, i if n == 0 else 0], h_recv.at[n, i],
             partner if n == 0 else z_from, s,
         )
 
@@ -568,8 +568,7 @@
 
     @pl.when(has_from)
     def _():
-        for c in hops_z:
-            c.wait_send()
+        remote(hop_out.at[1], hop_in.at[1], h_send.at[1, 0], h_recv.at[1, 0], z_from, s).wait_send()
 
 
 def body(n_genome, n_samp, dosage, effects, depth):

time: 109 us -> 109 us (level)
  no operation moved by 1% of the time
where the time goes in v8:
time: 109 us
  Pallas kernels  108 us (99%)
    pallas_call x1, Pallas kernels, body(): pl.pallas_call(functools.partial(kernel, n_genome, n_samp, nb, half, 1.0...  108 us

profile of v8, /device:TPU:0, one launch (start us, length us, event | category | flops | bytes accessed | tf_op | source)
XLA Modules:
  0.0 108.9 jit_solution(16816926858603782777)
XLA Ops:
  0.0 108.1 %shard_map.37 = f32[1024,128]{1,0:T(8,128)S(1)} custom-call(bf16[4096,1024]{1,0:T(8,128)(2,1)} %x_ref.1, bf16[1024,128]{1,0:T(8,128)(2,1)} %e_ref.1, s32[4]{0:T(128)} %depth_ref.1), custom_call_target="tpu_custom_call" | custom-call | flops 10737418240 | bytes 16777216 | tf_op jit(solution)/shard_map/pallas_call | solution.py:589
  108.1 0.8 copy.5
